TPU v7x, 512 devices: a whole 4x4x16 slice. The times are simulated.
512 devices in a mesh: slab: 32 (over z, x_hi), iface: 4 (over y), mech: 4 (over x_lo, core).
Axes of the slice: x: 4 (x_hi: 2, x_lo: 2; x = x_hi * 2 + x_lo), y: 4, z: 16, core: 2. Of those that a mesh axis runs over, the one named last changes fastest.
Arguments:
- temp_start: float32 [256, 4, 128, 512], P(('slab', 'mech'), 'iface'), may hold values from 0.5 to 3
- conductivity: float32 [256, 4, 128, 512], P(('slab', 'mech'), 'iface'), may hold values from 0.3 to 2.8
- gap_conductance: float32 [256, 4, 128], P(('slab', 'mech'), 'iface'), may hold values from 10 to 20
- partner: int32 [512], P('iface'), may hold values from 0 to 511, each once
- row_order: int32 [4, 128], P('iface'), may hold values from 0 to 127, each once within a row
- active_layers: int32 [4, 128], P('iface', ('slab', 'mech')), may hold values from 1 to 32, as said below
- trial_stress: float32 [256, 4, 128, 512], P(None, 'iface', ('slab', 'mech')), may hold values from 0.5 to 2
Outputs:
- stress: float32 [256, 4, 128, 512], P(None, 'iface', ('slab', 'mech'))
- element_strain: float32 [32, 4, 128, 512], P(None, 'iface', ('slab', 'mech'))
Inputs may be any that keep to these rules, and one draw needn't show every extreme that they name: `active_layers`: element layers that creep in one element row; some row has all 32.
All inputs are finite; a program needn't handle non-finite values.
Results may differ from a plain program's by a relative error of at most 0.00005.
Values sent between devices are 32-bit elements; how exact they have to be, the bound alone decides.
A program may use at most 64 MiB of HBM per device.

v0:
```python
import jax
import jax.numpy as jnp
from jax import lax
from jax.sharding import PartitionSpec as P

SWEEPS = 2
NEWTON = 4


FLUX_STEP = 0.03
CREEP_RATE = 200.0
ACTIVATION = 12.0
REFERENCE_TEMP = 1.0


def padded(block, sides, width):
    for axis, dim in sides:
        count = lax.axis_size(axis)
        forward = [(i, i + 1) for i in range(count - 1)]
        backward = [(target, source) for source, target in forward]
        low = lax.ppermute(
            lax.slice_in_dim(block, block.shape[dim] - width, None, axis=dim), axis, forward
        )
        high = lax.ppermute(lax.slice_in_dim(block, 0, width, axis=dim), axis, backward)
        block = jnp.concatenate([low, block, high], axis=dim)
    return block


def neighbour_weight(shift_z, shift_a, shift_r):
    reach = abs(shift_z) + abs(shift_a) + abs(shift_r)
    return [0.0, 1.0, 0.5, 0.25][reach]


def conduction(padded_temp, padded_cond):
    center_temp = padded_temp[1:-1, 1:-1, 1:-1]
    center_cond = padded_cond[1:-1, 1:-1, 1:-1]
    depth, across, radial = center_temp.shape
    radial_index = jnp.arange(radial, dtype=jnp.int32)
    gap_row = radial // 2
    outward_open = (radial_index != gap_row - 1).astype(jnp.float32)
    inward_open = (radial_index != gap_row).astype(jnp.float32)
    total = jnp.zeros(center_temp.shape, jnp.float32)
    for shift_z in (-1, 0, 1):
        for shift_a in (-1, 0, 1):
            for shift_r in (-1, 0, 1):
                if shift_z == 0 and shift_a == 0 and (shift_r == 0):
                    continue
                near_temp = padded_temp[
                    1 + shift_z : 1 + shift_z + depth,
                    1 + shift_a : 1 + shift_a + across,
                    1 + shift_r : 1 + shift_r + radial,
                ]
                near_cond = padded_cond[
                    1 + shift_z : 1 + shift_z + depth,
                    1 + shift_a : 1 + shift_a + across,
                    1 + shift_r : 1 + shift_r + radial,
                ]
                face = neighbour_weight(shift_z, shift_a, shift_r) * 0.5 * (center_cond + near_cond)
                if shift_r == 1:
                    face = face * outward_open
                elif shift_r == -1:
                    face = face * inward_open
                total = total + face * (near_temp - center_temp)
    return FLUX_STEP * total


def creep_return(mech_temp, trial, active_layers):
    rate = CREEP_RATE * jnp.exp(-ACTIVATION / (mech_temp + REFERENCE_TEMP))
    slip = jnp.zeros(trial.shape, jnp.float32)
    for newton_step in range(NEWTON):
        left = trial - slip
        residue = slip - rate * left**3
        slope = 1.0 + 3.0 * rate * left**2
        slip = slip - residue / slope
    depth = trial.shape[0]
    layer = jnp.arange(depth, dtype=jnp.int32) // 8
    live = (layer[:, None, None] < active_layers[None, :, :]).astype(jnp.float32)[..., None]
    creep = live * slip
    stress = trial - creep
    strain = jnp.sum(creep.reshape((depth // 8, 8) + trial.shape[1:]), axis=1) * 0.125
    return (stress, strain)


def on_device(
    temp_start, conductivity, gap_conductance, partner, row_order, active_layers, trial_stress
):
    depth = temp_start.shape[0]
    rows = temp_start.shape[2]
    radial = temp_start.shape[3]
    temp = temp_start.reshape(depth, rows, radial)
    cond = conductivity.reshape(depth, rows, radial)
    gap = gap_conductance.reshape(depth, rows)
    gap_row = radial // 2
    sections = lax.axis_size("iface")
    across = rows * sections
    all_cols = jnp.arange(across, dtype=jnp.int32)
    cond_rim = padded(cond, ((("slab", "mech"), 0), ("iface", 1)), 1)
    padded_cond = jnp.pad(cond_rim, ((0, 0), (0, 0), (1, 1)))
    spread_table = (partner[:, None] == all_cols[None, :]).astype(jnp.float32)
    for sweep in range(SWEEPS):
        temp_rim = padded(temp, ((("slab", "mech"), 0), ("iface", 1)), 1)
        padded_temp = jnp.pad(temp_rim, ((0, 0), (0, 0), (1, 1)))
        compact = temp[:, :, gap_row - 1]
        canister = temp[:, :, gap_row]
        compact_all = lax.all_gather(compact, "iface", axis=1, tiled=True)
        facing = jnp.take(compact_all, partner, axis=1)
        flux = gap * (facing - canister)
        spread = jnp.dot(
            flux, spread_table, precision=lax.Precision.HIGHEST, preferred_element_type=jnp.float32
        )
        returned = lax.psum_scatter(spread, "iface", scatter_dimension=1, tiled=True)
        fresh = temp + conduction(padded_temp, padded_cond)
        temp = (
            fresh.at[:, :, gap_row]
            .add(FLUX_STEP * flux)
            .at[:, :, gap_row - 1]
            .add(-FLUX_STEP * returned)
        )
    permuted = jnp.take(temp, row_order[0], axis=1)
    mech_temp = lax.all_to_all(permuted, ("slab", "mech"), split_axis=1, concat_axis=0, tiled=True)
    mech_temp = mech_temp.reshape(mech_temp.shape[0], 1, mech_temp.shape[1], radial)
    return creep_return(mech_temp, trial_stress, active_layers)


def solution(mesh):
    placed = (
        P(("slab", "mech"), "iface", None, None),
        P(("slab", "mech"), "iface", None, None),
        P(("slab", "mech"), "iface", None),
        P("iface"),
        P("iface", None),
        P("iface", ("slab", "mech")),
        P(None, "iface", ("slab", "mech"), None),
    )
    return jax.shard_map(
        on_device,
        mesh=mesh,
        in_specs=placed,
        out_specs=(
            P(None, "iface", ("slab", "mech"), None),
            P(None, "iface", ("slab", "mech"), None),
        ),
        check_vma=False,
    )
```

profile of v0, /device:TPU:1, one launch (start us, length us, event | category | flops | bytes accessed | tf_op | source)
XLA Modules:
  0.0 256.4 jit_solution(7770977692534962470)
XLA Ops:
  7.2 1.9 slice_bitcast_fusion.2
  9.2 4.5 %collective-permute-start = (f32[1,128,512]{2,1,0:T(8,128)}, f32[1,128,512]{2,1,0:T(8,128)S(1)}, u32[]{:S(2)}, u32[]{:S(2)}) collective-permute-start(f32[1,128,512]{2,1,0:T(8,128)} %get-tuple-element.100), channel_id=1, source_target_pairs={{0,1},{1,2},{2,3},{3,16},{16,17},{17,18},{18,19},{19,32},{32,33},{... | collective-permute-start | bytes 786440 | tf_op jit(solution)/shard_map/ppermute | solution.py:21
  13.7 5.6 %collective-permute-start.1 = (f32[1,128,512]{2,1,0:T(8,128)}, f32[1,128,512]{2,1,0:T(8,128)S(1)}, u32[]{:S(2)}, u32[]{:S(2)}) collective-permute-start(f32[1,128,512]{2,1,0:T(8,128)} %get-tuple-element.99), channel_id=1, source_target_pairs={{1,0},{2,1},{3,2},{16,3},{17,16},{18,17},{19,18},{32,19},{33,32},{... | collective-permute-start | bytes 786440 | tf_op jit(solution)/shard_map/ppermute | solution.py:24
  20.0 1.9 collective-permute-start.4
  21.9 2.4 collective-permute-start.5
  24.5 11.7 %all-gather = f32[2,512,1]{2,1,0:T(8,128)S(1)} all-gather(f32[2,128,1]{2,1,0:T(8,128)S(1)} %get-tuple-element.97), channel_id=2, replica_groups=mesh['slab'=32,'iface'=4,'mech'=4] {'iface'}, dimensions={1}, use_global_device_ids=true | all-gather | bytes 5120 | tf_op jit(solution)/shard_map/all_gather | solution.py:105
  36.3 3.1 %copy.918 = f32[2,512,1]{0,1,2:T(8,128)S(1)} copy(f32[2,512,1]{2,1,0:T(8,128)S(1)} %all-gather) | data formatting | bytes 8192 | tf_op jit(solution)/shard_map/all_gather | solution.py:105
  41.1 1.2 convolution_bitcast_fusion.1
  45.1 1.6 copy.888
  46.7 29.4 %reduce-scatter.7.cloned.1.call-done = f32[128,2]{1,0:T(8,128)} async-done(((f32[512,2]{1,0:T(8,128)}), f32[128,2]{1,0:T(8,128)}) %reduce-scatter.7.cloned.1.call-update) | async-done | bytes 1040
  77.9 1.4 collective-permute-start.2
  79.4 1.3 collective-permute-start.3
  80.8 4.0 %collective-permute-start.6 = (f32[4,1,512]{2,0,1:T(4,128)S(1)}, f32[4,1,512]{2,0,1:T(4,128)S(1)}, u32[]{:S(2)}, u32[]{:S(2)}) collective-permute-start(f32[4,1,512]{2,0,1:T(4,128)S(1)} %copy.876), channel_id=1, source_target_pairs={{0,4},{4,8},{8,12},{1,5},{5,9},{9,13},{2,6},{6,10},{10,14},{3,7},{... | collective-permute-start | bytes 24584 | tf_op jit(solution)/shard_map/ppermute | solution.py:21
  84.8 1.3 collective-permute-start.7
  86.7 1.4 pad_maximum_fusion
  88.2 1.0 collective-permute-done.7
  90.7 4.7 %fusion.80 = f32[2,128,512]{2,1,0:T(8,128)S(1)} fusion(f32[2,128,512]{2,1,0:T(8,128)S(1)} %bitcast.82, f32[4,130,514]{2,1,0:T(8,128)S(1)} %select_maximum_fusion.4, f32[4,129,512]{2,1,0:T(8,128)S(1)} %get-tuple-element.92, f32[1,128,512]{2,1,0:T(8,128)S(1)} %copy-done.14, f32[4,129,512]{2,1,0:T(8,128)S(1)} %get-tuple-element.91, ...), kind=kLoop, calls=%fused_computation.140 | loop fusion | flops 17694720 | bytes 27799552 | tf_op jit(solution)/shard_map/add | solution.py:112
  96.1 1.1 scatter-add.14
  97.3 1.0 slice_add_fusion.26
  98.9 11.7 %all-gather.1 = f32[2,512,1]{2,1,0:T(8,128)} all-gather(f32[2,128,1]{2,1,0:T(8,128)S(1)} %slice_add_fusion.26), channel_id=3, replica_groups=mesh['slab'=32,'iface'=4,'mech'=4] {'iface'}, dimensions={1}, use_global_device_ids=true | all-gather | bytes 5120 | tf_op jit(solution)/shard_map/all_gather | solution.py:105
  110.7 1.3 scatter-add.15
  113.5 4.8 %copy.922 = f32[2,512,1]{0,1,2:T(8,128)} copy(f32[2,512,1]{2,1,0:T(8,128)} %all-gather.1) | data formatting | bytes 8192 | tf_op jit(solution)/shard_map/all_gather | solution.py:105
  118.3 2.3 gather_fusion.2
  120.7 2.4 copy.923
  123.0 9.5 %collective-permute-start.8 = (f32[1,128,512]{2,1,0:T(8,128)}, f32[1,128,512]{2,1,0:T(8,128)}, u32[]{:S(2)}, u32[]{:S(2)}) collective-permute-start(f32[1,128,512]{2,1,0:T(8,128)} %get-tuple-element.95), channel_id=1, source_target_pairs={{0,1},{1,2},{2,3},{3,16},{16,17},{17,18},{18,19},{19,32},{32,33},{... | collective-permute-start | bytes 786440 | tf_op jit(solution)/shard_map/ppermute | solution.py:21
  132.5 2.1 collective-permute-start.9
  134.6 1.6 multiply_bitcast_fusion.2
  136.2 1.8 convolution_bitcast_fusion
  138.1 1.2 pad_clamp_fusion
  139.3 2.4 copy.899
  141.7 23.5 %reduce-scatter.9.cloned.1.call-done = f32[128,2]{1,0:T(8,128)} async-done(((f32[512,2]{1,0:T(8,128)}), f32[128,2]{1,0:T(8,128)}) %reduce-scatter.9.cloned.1.call-update) | async-done | bytes 1040
  165.1 1.4 copy.929
  168.0 2.0 collective-permute-start.10
  170.6 1.5 collective-permute-start.11
  172.1 1.1 multiply_bitcast_fusion.4
  173.2 1.4 copy.900
  176.1 1.5 maximum_maximum_fusion.2
  177.7 1.6 select_maximum_fusion
  179.4 5.7 %fusion.25 = f32[2,128,512]{2,1,0:T(8,128)S(1)} fusion(f32[2,128,512]{2,1,0:T(8,128)S(1)} %scatter-add.15, f32[4,130,514]{2,1,0:T(8,128)S(1)} %select_maximum_fusion, f32[4,129,512]{2,1,0:T(8,128)S(1)} %get-tuple-element.84, f32[1,128,512]{2,1,0:T(8,128)} %collective-permute-done.9, f32[4,129,512]{2,1,0:T(8,128)S(1)} %get-tuple-element.83, ...), kind=kLoop, calls=%fused_computation.59 | loop fusion | flops 17694720 | bytes 27799552 | tf_op jit(solution)/shard_map/add | solution.py:112
  186.0 1.6 scatter-add.16
  187.6 1.1 slice_add_fusion.24
  188.6 1.8 scatter-add.19
  190.4 1.4 copy.901
  191.9 1.3 gather_fusion
  193.1 1.1 select_bitcast_fusion
  194.2 20.0 %all-to-all-start = ((f32[2,128,512]{2,0,1:T(2,128)}), f32[2,128,512]{2,0,1:T(2,128)S(1)}, u32[]{:S(2)}, u32[]{:S(2)}) async-start(f32[2,128,512]{2,0,1:T(2,128)} %select_bitcast_fusion), calls=%async_computation | async-start | bytes 1048576 | tf_op jit(solution)/shard_map/all_to_all | solution.py:120
  214.9 30.2 %all-to-all-done = f32[2,128,512]{2,0,1:T(2,128)S(1)} async-done(((f32[2,128,512]{2,0,1:T(2,128)}), f32[2,128,512]{2,0,1:T(2,128)S(1)}, u32[]{:S(2)}, u32[]{:S(2)}) %all-to-all-start) | async-done | bytes 524320 | tf_op jit(solution)/shard_map/all_to_all | solution.py:120
  247.6 1.3 copy.917
  (141 shorter events, 19.4 us)
Async XLA Ops:
  7.2 12.1 %copy-start.3 = (f32[2,1,128,512]{3,2,1,0:T(8,128)S(1)}, f32[2,1,128,512]{3,2,1,0:T(8,128)}, u32[]{:S(2)}) copy-start(f32[2,1,128,512]{3,2,1,0:T(8,128)} %param.17) | copy-start | bytes 1572868
  7.2 17.2 %copy-start.34 = (s32[128]{0:T(128)S(1)}, s32[128]{0:T(128)}, u32[]{:S(2)}) copy-start(s32[128]{0:T(128)} %param.20) | copy-start | bytes 1540
  7.2 68.9 %reduce-scatter.7.cloned.1.call-start = ((), (), s32[]{:S(2)}) async-start(), calls=%async_computation.3 | async-start | bytes 327680
  9.2 68.7 %collective-permute-start = (f32[1,128,512]{2,1,0:T(8,128)}, f32[1,128,512]{2,1,0:T(8,128)S(1)}, u32[]{:S(2)}, u32[]{:S(2)}) collective-permute-start(f32[1,128,512]{2,1,0:T(8,128)} %get-tuple-element.100), channel_id=1, source_target_pairs={{0,1},{1,2},{2,3},{3,16},{16,17},{17,18},{18,19},{19,32},{32,33},{... | collective-permute-start | bytes 786440 | tf_op jit(solution)/shard_map/ppermute | solution.py:21
  13.7 26.6 %copy-start.36 = (f32[2,1,128]{2,1,0:T(1,128)S(1)}, f32[2,1,128]{2,1,0:T(1,128)}, u32[]{:S(2)}) copy-start(f32[2,1,128]{2,1,0:T(1,128)} %param.19) | copy-start | bytes 3076
  13.7 64.2 %collective-permute-start.1 = (f32[1,128,512]{2,1,0:T(8,128)}, f32[1,128,512]{2,1,0:T(8,128)S(1)}, u32[]{:S(2)}, u32[]{:S(2)}) collective-permute-start(f32[1,128,512]{2,1,0:T(8,128)} %get-tuple-element.99), channel_id=1, source_target_pairs={{1,0},{2,1},{3,2},{16,3},{17,16},{18,17},{19,18},{32,19},{33,32},{... | collective-permute-start | bytes 786440 | tf_op jit(solution)/shard_map/ppermute | solution.py:24
  20.0 60.7 %collective-permute-start.4 = (f32[1,128,512]{2,1,0:T(8,128)}, f32[1,128,512]{2,1,0:T(8,128)S(1)}, u32[]{:S(2)}, u32[]{:S(2)}) collective-permute-start(f32[1,128,512]{2,1,0:T(8,128)} %get-tuple-element.101), channel_id=1, source_target_pairs={{0,1},{1,2},{2,3},{3,16},{16,17},{17,18},{18,19},{19,32},{32,33},{... | collective-permute-start | bytes 786440 | tf_op jit(solution)/shard_map/ppermute | solution.py:21
  21.9 58.8 %collective-permute-start.5 = (f32[1,128,512]{2,1,0:T(8,128)S(1)}, f32[1,128,512]{2,1,0:T(8,128)S(1)}, u32[]{:S(2)}, u32[]{:S(2)}) collective-permute-start(f32[1,128,512]{2,1,0:T(8,128)S(1)} %get-tuple-element.102), channel_id=1, source_target_pairs={{1,0},{2,1},{3,2},{16,3},{17,16},{18,17},{19,18},{32,19},{33,32},{... | collective-permute-start | bytes 786440 | tf_op jit(solution)/shard_map/ppermute | solution.py:24
  24.4 17.9 %copy-start.35 = (pred[128]{0:T(512)(128)(4,1)}, pred[128]{0:T(512)(128)(4,1)S(1)}, u32[]{:S(2)}) copy-start(pred[128]{0:T(512)(128)(4,1)S(1)} %compare_and_fusion) | copy-start | bytes 388
  24.5 19.0 %copy-start.38 = (s32[1,128]{1,0:T(1,128)S(1)}, s32[1,128]{1,0:T(1,128)}, u32[]{:S(2)}) copy-start(s32[1,128]{1,0:T(1,128)} %param.21) | copy-start | bytes 1540
  24.5 53.4 %copy-start = (f32[2,1,128,512]{3,2,1,0:T(8,128)S(1)}, f32[2,1,128,512]{3,2,1,0:T(8,128)}, u32[]{:S(2)}) copy-start(f32[2,1,128,512]{3,2,1,0:T(8,128)} %param.18) | copy-start | bytes 1572868
  39.4 41.4 %copy-start.33 = (s32[1024]{0:T(1024)}, s32[1024]{0:T(1024)S(1)}, u32[]{:S(2)}) copy-start(s32[1024]{0:T(1024)S(1)} %pad_clamp_fusion.1) | copy-start | bytes 12292
  40.4 40.4 %copy-start.18 = (f32[2,1,128]{0,2,1:T(8,128)}, f32[2,1,128]{0,2,1:T(8,128)S(1)}, u32[]{:S(2)}) copy-start(f32[2,1,128]{0,2,1:T(8,128)S(1)} %copy.884) | copy-start | bytes 3076
  42.3 122.8 %reduce-scatter.9.cloned.1.call-start = ((), (), s32[]{:S(2)}) async-start(), calls=%async_computation.4 | async-start | bytes 327680
  77.9 8.3 %copy-start.5 = (f32[1,128,512]{2,1,0:T(8,128)}, f32[1,128,512]{2,1,0:T(8,128)S(1)}, u32[]{:S(2)}) copy-start(f32[1,128,512]{2,1,0:T(8,128)S(1)} %collective-permute-done) | copy-start | bytes 786436
  77.9 8.3 %copy-start.8 = (f32[1,128,512]{2,1,0:T(8,128)}, f32[1,128,512]{2,1,0:T(8,128)S(1)}, u32[]{:S(2)}) copy-start(f32[1,128,512]{2,1,0:T(8,128)S(1)} %collective-permute-done.1) | copy-start | bytes 786436
  77.9 8.2 %collective-permute-start.2 = (f32[4,1,512]{2,0,1:T(4,128)S(1)}, f32[4,1,512]{2,0,1:T(4,128)S(1)}, u32[]{:S(2)}, u32[]{:S(2)}) collective-permute-start(f32[4,1,512]{2,0,1:T(4,128)S(1)} %copy.872), channel_id=1, source_target_pairs={{0,4},{4,8},{8,12},{1,5},{5,9},{9,13},{2,6},{6,10},{10,14},{3,7},{... | collective-permute-start | bytes 24584 | tf_op jit(solution)/shard_map/ppermute | solution.py:21
  79.4 6.7 %collective-permute-start.3 = (f32[4,1,512]{2,0,1:T(4,128)S(1)}, f32[4,1,512]{2,0,1:T(4,128)S(1)}, u32[]{:S(2)}, u32[]{:S(2)}) collective-permute-start(f32[4,1,512]{2,0,1:T(4,128)S(1)} %copy.873), channel_id=1, source_target_pairs={{4,0},{8,4},{12,8},{5,1},{9,5},{13,9},{6,2},{10,6},{14,10},{7,3},{... | collective-permute-start | bytes 24584 | tf_op jit(solution)/shard_map/ppermute | solution.py:24
  80.7 5.4 %copy-start.11 = (f32[1,128,512]{2,1,0:T(8,128)}, f32[1,128,512]{2,1,0:T(8,128)S(1)}, u32[]{:S(2)}) copy-start(f32[1,128,512]{2,1,0:T(8,128)S(1)} %collective-permute-done.4) | copy-start | bytes 786436
  80.7 5.4 %copy-start.13 = (f32[1,128,512]{2,1,0:T(8,128)}, f32[1,128,512]{2,1,0:T(8,128)S(1)}, u32[]{:S(2)}) copy-start(f32[1,128,512]{2,1,0:T(8,128)S(1)} %collective-permute-done.5) | copy-start | bytes 786436
  80.8 7.4 %collective-permute-start.6 = (f32[4,1,512]{2,0,1:T(4,128)S(1)}, f32[4,1,512]{2,0,1:T(4,128)S(1)}, u32[]{:S(2)}, u32[]{:S(2)}) collective-permute-start(f32[4,1,512]{2,0,1:T(4,128)S(1)} %copy.876), channel_id=1, source_target_pairs={{0,4},{4,8},{8,12},{1,5},{5,9},{9,13},{2,6},{6,10},{10,14},{3,7},{... | collective-permute-start | bytes 24584 | tf_op jit(solution)/shard_map/ppermute | solution.py:21
  84.8 4.4 %collective-permute-start.7 = (f32[4,1,512]{2,0,1:T(4,128)S(1)}, f32[4,1,512]{2,0,1:T(4,128)S(1)}, u32[]{:S(2)}, u32[]{:S(2)}) collective-permute-start(f32[4,1,512]{2,0,1:T(4,128)S(1)} %copy.877), channel_id=1, source_target_pairs={{4,0},{8,4},{12,8},{5,1},{9,5},{13,9},{6,2},{10,6},{14,10},{7,3},{... | collective-permute-start | bytes 24584 | tf_op jit(solution)/shard_map/ppermute | solution.py:24
  86.7 2.5 copy-start.12
  86.7 2.5 copy-start.14
  88.2 1.9 copy-start.1
  89.5 1.2 copy-start.9
  89.5 1.2 copy-start.21
  89.5 1.2 copy-start.23
  89.5 1.1 copy-start.25
  89.5 1.1 copy-start.27
  89.5 1.1 copy-start.29
  90.7 4.7 %copy-start.19 = (f32[2,128,1]{2,1,0:T(8,128)S(1)}, f32[2,128,1]{2,1,0:T(8,128)}, u32[]{:S(2)}) copy-start(f32[2,128,1]{2,1,0:T(8,128)} %copy.888) | copy-start | bytes 3076
  123.0 43.6 %collective-permute-start.8 = (f32[1,128,512]{2,1,0:T(8,128)}, f32[1,128,512]{2,1,0:T(8,128)}, u32[]{:S(2)}, u32[]{:S(2)}) collective-permute-start(f32[1,128,512]{2,1,0:T(8,128)} %get-tuple-element.95), channel_id=1, source_target_pairs={{0,1},{1,2},{2,3},{3,16},{16,17},{17,18},{18,19},{19,32},{32,33},{... | collective-permute-start | bytes 786440 | tf_op jit(solution)/shard_map/ppermute | solution.py:21
  132.5 34.1 %collective-permute-start.9 = (f32[1,128,512]{2,1,0:T(8,128)}, f32[1,128,512]{2,1,0:T(8,128)}, u32[]{:S(2)}, u32[]{:S(2)}) collective-permute-start(f32[1,128,512]{2,1,0:T(8,128)} %get-tuple-element.96), channel_id=1, source_target_pairs={{1,0},{2,1},{3,2},{16,3},{17,16},{18,17},{19,18},{32,19},{33,32},{... | collective-permute-start | bytes 786440 | tf_op jit(solution)/shard_map/ppermute | solution.py:24
  168.0 6.7 %collective-permute-start.10 = (f32[4,1,512]{2,0,1:T(4,128)}, f32[4,1,512]{2,0,1:T(4,128)}, u32[]{:S(2)}, u32[]{:S(2)}) collective-permute-start(f32[4,1,512]{2,0,1:T(4,128)} %copy.890), channel_id=1, source_target_pairs={{0,4},{4,8},{8,12},{1,5},{5,9},{9,13},{2,6},{6,10},{10,14},{3,7},{... | collective-permute-start | bytes 24584 | tf_op jit(solution)/shard_map/ppermute | solution.py:21
  170.6 4.7 %collective-permute-start.11 = (f32[4,1,512]{2,0,1:T(4,128)}, f32[4,1,512]{2,0,1:T(4,128)}, u32[]{:S(2)}, u32[]{:S(2)}) collective-permute-start(f32[4,1,512]{2,0,1:T(4,128)} %copy.891), channel_id=1, source_target_pairs={{4,0},{8,4},{12,8},{5,1},{9,5},{13,9},{6,2},{10,6},{14,10},{7,3},{... | collective-permute-start | bytes 24584 | tf_op jit(solution)/shard_map/ppermute | solution.py:24
  177.6 1.7 copy-start.2
  177.6 1.7 copy-start.7
  177.6 1.7 copy-start.10
  177.6 1.7 copy-start.22
  177.6 1.7 copy-start.24
  177.6 1.7 copy-start.26
  177.6 1.7 copy-start.28
  177.6 1.7 copy-start.30
  177.6 1.7 copy-start.32
  179.4 6.5 %copy-start.20 = (f32[2,128,1]{2,1,0:T(8,128)S(1)}, f32[2,128,1]{2,1,0:T(8,128)}, u32[]{:S(2)}) copy-start(f32[2,128,1]{2,1,0:T(8,128)} %copy.899) | copy-start | bytes 3076
  187.6 5.6 %copy-start.37 = (pred[128]{0:T(512)(128)(4,1)S(1)}, pred[128]{0:T(512)(128)(4,1)}, u32[]{:S(2)}) copy-start(pred[128]{0:T(512)(128)(4,1)} %compare_and_fusion.1) | copy-start | bytes 388
  194.2 50.8 %all-to-all-start = ((f32[2,128,512]{2,0,1:T(2,128)}), f32[2,128,512]{2,0,1:T(2,128)S(1)}, u32[]{:S(2)}, u32[]{:S(2)}) async-start(f32[2,128,512]{2,0,1:T(2,128)} %select_bitcast_fusion), calls=%async_computation | async-start | bytes 1048576 | tf_op jit(solution)/shard_map/all_to_all | solution.py:120
  (6 other events, 5.8 us)
Sparse Core Ops, SparseCore 0:
  42.4 33.6 reduce-scatter.6
  138.2 26.8 reduce-scatter.8
where the time goes:
time: 259 us; the launch traced here: 256 us
  waiting for transfers between devices  84.1 us (32%)
  starting transfers between devices  57.6 us (22%)
  local copies, waits for them, and re-layouts  43.3 us (17%)
  other arithmetic  29.4 us (11%)
  blocking collectives  23.5 us (9%)
  between operations  15.6 us (6%)
  matrix products  3.01 us (1%)
    unnamed x4, waiting for transfers between devices  52.9 us
    all_to_all x1, waiting for transfers between devices, on_device(): lax.all_to_all(permuted, ('slab', 'mech'), split_axis=1, concat_axis=0, t...  30.2 us
    all_gather x2, blocking collectives, on_device(): compact_all = lax.all_gather(compact, 'iface', axis=1, tiled=True)  23.5 us
    ppermute x6, starting transfers between devices, padded(): lax.ppermute(lax.slice_in_dim(block, block.shape[dim] - width, None, axis...  23.3 us
    all_to_all x1, starting transfers between devices, on_device(): lax.all_to_all(permuted, ('slab', 'mech'), split_axis=1, concat_axis=0, t...  20 us
    ppermute x6, starting transfers between devices, padded(): lax.ppermute(lax.slice_in_dim(block, 0, width, axis=dim), axis, backward)  14.2 us
    add x2, other arithmetic, on_device(): fresh = temp + conduction(padded_temp, padded_cond)  10.5 us
    all_gather x2, local copies, waits for them, and re-layouts, on_device(): compact_all = lax.all_gather(compact, 'iface', axis=1, tiled=True)  7.95 us
  transfers between devices with their start and end apart: 15, of which 4 were waited for; matrix products, arithmetic and copies ran while one was open for 11% of the time, Pallas kernels for 0%

commit v1 on v0

v1 whole, which is shorter than its diff:
```python
import functools

import jax
import jax.numpy as jnp
from jax import lax
from jax.experimental import pallas as pl
from jax.experimental.pallas import tpu as pltpu
from jax.sharding import PartitionSpec as P

MESH = pl.DeviceIdType.MESH
NEWTON = 4
STEP = 0.03
CREEP_RATE = 200.0
ACTIVATION = 12.0
REFERENCE_TEMP = 1.0
LANES = 128
PAD = 8
CHUNK = 32


def kernel(
    slabs,
    sections,
    mechs,
    temp_ref,
    cond_ref,
    gap_ref,
    partner_ref,
    order_ref,
    active_ref,
    trial_ref,
    stress_ref,
    strain_ref,
    own_t,
    own_k,
    halo,
    fresh,
    halo2,
    u,
    keep,
    addend,
    cols,
    xbuf,
    hot,
    edge_out,
    edge_in,
    corner_in,
    edge_out2,
    edge_in2,
    corner_in2,
    packed,
    send,
    recv,
    trial_v,
    stress_v,
    strain_v,
    load_sem,
    out_sem,
    send_sem,
    layer_sem,
    edge_sem,
    corner_sem,
    layer2_sem,
    edge2_sem,
    corner2_sem,
    spread_send_sem,
    spread_sem,
    ready_sem,
):
    n = slabs * mechs
    group = 2 * mechs
    groups = n // group
    rows = own_t.shape[1]
    me = lax.axis_index("slab") * mechs + lax.axis_index("mech")
    y = lax.axis_index("iface")
    mine, place = me // group, me % group
    below, above = (me + n - 1) % n, (me + 1) % n
    y_low, y_high, y_far = (y + sections - 1) % sections, (y + 1) % sections, (y + 2) % sections

    def device(k, section):
        return (k // mechs, section, k % mechs)

    load_t = pltpu.make_async_copy(temp_ref, own_t, load_sem.at[0])
    load_k = pltpu.make_async_copy(cond_ref, own_k, load_sem.at[1])
    load_trial = pltpu.make_async_copy(trial_ref, trial_v, load_sem.at[2])
    load_t.start()
    load_k.start()

    barrier = pltpu.get_barrier_semaphore()

    def greet(k, section):
        pl.semaphore_signal(barrier, inc=1, device_id=device(k, section), device_id_type=MESH)

    near = [
        (below, y), (above, y), (me, y_low), (me, y_high), (me, y_far),
        (below, y_low), (below, y_high), (above, y_low), (above, y_high),
    ]
    for k, section in near:
        greet(k, section)
    for step in range(1, group):
        greet(mine * group + (place + step) % group, y)
    for step in range(1, groups):
        greet(((mine + step) % groups) * group + place, y)

    load_trial.start()
    row_of = lax.broadcasted_iota(jnp.int32, (rows, LANES), 0)
    lane_of = lax.broadcasted_iota(jnp.int32, (rows, LANES), 1)
    diagonal = row_of == lane_of

    def as_row(column):
        return jnp.sum(jnp.where(diagonal, column, 0.0), axis=0, keepdims=True)

    def as_column(row):
        return jnp.sum(jnp.where(diagonal, row, 0.0), axis=1, keepdims=True)

    base = (y * rows).astype(jnp.float32)
    whole = float(sections * rows)

    def relative(index):
        shifted = index - base
        return jnp.where(shifted < 0.0, shifted + whole, shifted)

    partner_row = partner_ref[...].astype(jnp.float32)
    partner_column = as_column(relative(partner_row))
    cols[:, 0:1] = as_column(gap_ref[0:1, :])
    cols[:, 1:2] = as_column(gap_ref[1:2, :])
    for q in range(sections):
        at = lax.broadcasted_iota(jnp.int32, (rows, LANES), 1).astype(jnp.float32) + float(q * rows)
        hot[0:rows, q * LANES : (q + 1) * LANES] = jnp.where(at == partner_column, 1.0, 0.0).astype(jnp.bfloat16)
    load_t.wait()
    load_k.wait()
    zeros_row = jnp.zeros((1, LANES), jnp.float32)
    for e, at in ((0, 0), (1, rows - 1)):
        for layer in range(2):
            edge_out[e, layer : layer + 1, :] = own_t[layer, at : at + 1, :]
            edge_out[e, 2 + layer : 3 + layer, :] = own_k[layer, at : at + 1, :]
    for layer in range(2):
        compact = as_row(own_t[layer, :, 2 * LANES - 1 : 2 * LANES])
        canister = as_row(own_t[layer, :, 2 * LANES : 2 * LANES + 1])
        for e in range(2):
            edge_out[e, 4:5, layer * LANES : (layer + 1) * LANES] = compact
            edge_out[e, 4:5, (2 + layer) * LANES : (3 + layer) * LANES] = canister
            edge_out[e, 5:6, layer * LANES : (layer + 1) * LANES] = gap_ref[layer : layer + 1, :]
    for e in range(2):
        edge_out[e, 5:6, 2 * LANES : 3 * LANES] = partner_row
        edge_out[e, 5:6, 3 * LANES : 4 * LANES] = zeros_row
        edge_out[e, 6:8, :] = jnp.zeros((2, 4 * LANES), jnp.float32)
        edge_out2[e] = jnp.zeros((8, 4 * LANES), jnp.float32)
    pl.semaphore_wait(barrier, len(near) + group - 1 + groups - 1)

    for step in range(1, groups):
        pl.semaphore_signal(
            ready_sem, inc=1, device_id=device(((mine + step) % groups) * group + place, y), device_id_type=MESH
        )

    def remote(source, target, sent, landed, k, section):
        return pltpu.make_async_remote_copy(
            src_ref=source, dst_ref=target, send_sem=sent, recv_sem=landed,
            device_id=device(k, section), device_id_type=MESH,
        )

    def edge_copies(out, into, corners, edge_landed, corner_landed, first):
        return [
            remote(out.at[1], into.at[0], send_sem.at[first], edge_landed.at[0], me, y_high),
            remote(out.at[0], into.at[1], send_sem.at[first + 1], edge_landed.at[1], me, y_low),
            remote(out.at[0], into.at[2], send_sem.at[first + 2], edge_landed.at[2], me, y_far),
            remote(out.at[1], corners.at[0, 0], send_sem.at[first + 3], corner_landed.at[0], above, y_high),
            remote(out.at[0], corners.at[0, 1], send_sem.at[first + 4], corner_landed.at[1], above, y_low),
            remote(out.at[1], corners.at[1, 0], send_sem.at[first + 5], corner_landed.at[2], below, y_high),
            remote(out.at[0], corners.at[1, 1], send_sem.at[first + 6], corner_landed.at[3], below, y_low),
        ]

    edges = edge_copies(edge_out, edge_in, corner_in, edge_sem, corner_sem, 0)
    for copy in edges:
        copy.start()
    layers = [
        remote(temp_ref.at[0], halo.at[1, 0], send_sem.at[7], layer_sem.at[1, 0], below, y),
        remote(temp_ref.at[1], halo.at[0, 0], send_sem.at[8], layer_sem.at[0, 0], above, y),
        remote(cond_ref.at[0], halo.at[1, 1], send_sem.at[9], layer_sem.at[1, 1], below, y),
        remote(cond_ref.at[1], halo.at[0, 1], send_sem.at[10], layer_sem.at[0, 1], above, y),
    ]
    for copy in layers:
        copy.start()

    has_below = jnp.where(me > 0, 0.5, 0.0).astype(jnp.float32)
    has_above = jnp.where(me < n - 1, 0.5, 0.0).astype(jnp.float32)
    has_low = jnp.where(y > 0, 1.0, 0.0).astype(jnp.float32)
    has_high = jnp.where(y < sections - 1, 1.0, 0.0).astype(jnp.float32)

    def across_layers(before, first, second, after):
        return (
            first + 0.5 * second + has_below * before,
            second + 0.5 * first + has_above * after,
        )

    def fill_edges(t_of, k_of, with_cond):
        for e, row, there in ((0, PAD - 1, has_low), (1, PAD + rows, has_high)):
            ts, ks = t_of(e), k_of(e)
            sums = [across_layers(*ts), across_layers(*[a * b for a, b in zip(ts, ks)])]
            if with_cond:
                sums.append(across_layers(*ks))
            for f, pair in enumerate(sums):
                for layer in range(2):
                    edge = there * pair[layer]
                    for c in range(4):
                        u[layer, f, c, row : row + 1, :] = edge[:, c * LANES : (c + 1) * LANES]

    def fill_rows(t_of, k_of, with_cond):
        def body(i, carry):
            start = pl.multiple_of(i * CHUNK, CHUNK)
            at = pl.ds(start, CHUNK)
            to = pl.ds(pl.multiple_of(start + PAD, 8), CHUNK)
            for c in range(4):
                ts, ks = t_of(at, c), k_of(at, c)
                sums = [across_layers(*ts), across_layers(*[a * b for a, b in zip(ts, ks)])]
                if with_cond:
                    sums.append(across_layers(*ks))
                for f, pair in enumerate(sums):
                    for layer in range(2):
                        u[layer, f, c, to, :] = pair[layer]
            return carry

        lax.fori_loop(0, rows // CHUNK, body, 0)

    lane = lax.broadcasted_iota(jnp.int32, (CHUNK, LANES), 1)
    first_lane, last_lane = lane == 0, lane == LANES - 1

    def spread_of(layer, f, c0, start):
        v = []
        for c in (c0, c0 + 1):
            mid = u[layer, f, c, pl.ds(start + PAD, CHUNK), :]
            up = u[layer, f, c, pl.ds(start + PAD - 1, CHUNK), :]
            down = u[layer, f, c, pl.ds(start + PAD + 1, CHUNK), :]
            v.append(mid + 0.5 * (up + down))
        right = [pltpu.roll(x, 1, 1) for x in v]
        left = [pltpu.roll(x, LANES - 1, 1) for x in v]
        return [
            v[0] + 0.5 * (jnp.where(first_lane, 0.0, right[0]) + jnp.where(last_lane, left[1], left[0])),
            v[1] + 0.5 * (jnp.where(first_lane, right[0], right[1]) + jnp.where(last_lane, 0.0, left[1])),
        ]

    def sweep(t_of, put, first):
        for layer in range(2):
            for half in range(2):
                for i in range(rows // CHUNK):
                    start = i * CHUNK
                    at = pl.ds(start, CHUNK)
                    spread_t = spread_of(layer, 0, 2 * half, start)
                    spread_kt = spread_of(layer, 1, 2 * half, start)
                    spread_k = spread_of(layer, 2, 2 * half, start) if first else None
                    for j in range(2):
                        c = 2 * half + j
                        k = own_k[layer, at, c * LANES : (c + 1) * LANES]
                        t = t_of(layer, at, c)
                        if first:
                            weight = jnp.full((CHUNK, LANES), 8.0, jnp.float32)
                            if c == 1:
                                weight = jnp.where(last_lane, 6.0, weight)
                            if c == 2:
                                weight = jnp.where(first_lane, 6.0, weight)
                            drain = weight * k + spread_k[j]
                            keep[layer, c, at, :] = drain
                        else:
                            drain = keep[layer, c, at, :]
                        new = t + STEP * (k * spread_t[j] + spread_kt[j] - t * drain)
                        if c in (1, 2):
                            new = new + addend[layer, c - 1, at, :]
                        put(layer, c, start, new)

    def gather(faces, into, slots):
        for q, block in enumerate([faces[0], *[into[s] for s in slots]]):
            for layer in range(4):
                xbuf[layer : layer + 1, q * LANES : (q + 1) * LANES] = block[4:5, layer * LANES : (layer + 1) * LANES]
            for layer in range(2):
                xbuf[4 + layer : 5 + layer, q * LANES : (q + 1) * LANES] = block[
                    5:6, layer * LANES : (layer + 1) * LANES
                ]
        x = xbuf[...]
        high = x.astype(jnp.bfloat16)
        rest = x - high.astype(jnp.float32)
        middle = rest.astype(jnp.bfloat16)
        low = (rest - middle.astype(jnp.float32)).astype(jnp.bfloat16)
        return sum(
            lax.dot_general(hot[...], part, (((1,), (1,)), ((), ())), preferred_element_type=jnp.float32)
            for part in (high, middle, low)
        )

    def gap_flux(found, face_of):
        for layer in range(2):
            compact, canister = face_of(layer)
            flux = cols[:, layer : layer + 1] * (found[0:rows, layer : layer + 1] - canister)
            returned = cols[:, 2 + layer : 3 + layer] * (compact - found[rows : 2 * rows, 2 + layer : 3 + layer])
            addend[layer, 0] = jnp.where(lane_of == LANES - 1, -STEP * returned, 0.0)
            addend[layer, 1] = jnp.where(lane_of == 0, STEP * flux, 0.0)

    xbuf[6:8, :] = jnp.zeros((2, 4 * LANES), jnp.float32)
    for copy in edges[:3]:
        copy.wait_recv()
    slots = (1, 2, 0)
    for q, block in enumerate([edge_out[0], *[edge_in[s] for s in slots]]):
        theirs = relative(block[5:6, 2 * LANES : 3 * LANES])
        hot[rows : 2 * rows, q * LANES : (q + 1) * LANES] = jnp.where(
            row_of.astype(jnp.float32) == theirs, 1.0, 0.0
        ).astype(jnp.bfloat16)
    found = gather(edge_out, edge_in, slots)
    cols[:, 2:4] = found[rows : 2 * rows, 4:6]
    gap_flux(
        found,
        lambda layer: (own_t[layer, :, 2 * LANES - 1 : 2 * LANES], own_t[layer, :, 2 * LANES : 2 * LANES + 1]),
    )
    for copy in edges[3:]:
        copy.wait_recv()

    def edge_layers(into, corners, row):
        def of(e):
            return (
                corners[0, e, row + 1 : row + 2, :],
                into[e, row : row + 1, :],
                into[e, row + 1 : row + 2, :],
                corners[1, e, row : row + 1, :],
            )

        return of

    fill_edges(edge_layers(edge_in, corner_in, 0), edge_layers(edge_in, corner_in, 2), True)
    for copy in layers:
        copy.wait_recv()

    def block(c):
        return slice(c * LANES, (c + 1) * LANES)

    def k_rows(at, c):
        return (halo[0, 1, at, block(c)], own_k[0, at, block(c)], own_k[1, at, block(c)], halo[1, 1, at, block(c)])

    fill_rows(
        lambda at, c: (halo[0, 0, at, block(c)], own_t[0, at, block(c)], own_t[1, at, block(c)], halo[1, 0, at, block(c)]),
        k_rows,
        True,
    )

    def put_fresh(layer, c, start, new):
        fresh[layer, c, pl.ds(start, CHUNK), :] = new

    sweep(lambda layer, at, c: own_t[layer, at, block(c)], put_fresh, True)

    layers2 = [
        remote(fresh.at[0], halo2.at[1], send_sem.at[18], layer2_sem.at[1], below, y),
        remote(fresh.at[1], halo2.at[0], send_sem.at[19], layer2_sem.at[0], above, y),
    ]
    for copy in layers2:
        copy.start()
    for e, at in ((0, 0), (1, rows - 1)):
        for layer in range(2):
            for c in range(4):
                edge_out2[e, layer : layer + 1, block(c)] = fresh[layer, c, at : at + 1, :]
    for layer in range(2):
        compact = as_row(fresh[layer, 1, :, LANES - 1 : LANES])
        canister = as_row(fresh[layer, 2, :, 0:1])
        for e in range(2):
            edge_out2[e, 4:5, layer * LANES : (layer + 1) * LANES] = compact
            edge_out2[e, 4:5, (2 + layer) * LANES : (3 + layer) * LANES] = canister
    edges2 = edge_copies(edge_out2, edge_in2, corner_in2, edge2_sem, corner2_sem, 11)
    for copy in edges2:
        copy.start()

    for copy in edges2[:3]:
        copy.wait_recv()
    found = gather(edge_out2, edge_in2, slots)
    gap_flux(found, lambda layer: (fresh[layer, 1, :, LANES - 1 : LANES], fresh[layer, 2, :, 0:1]))
    for copy in edges2[3:]:
        copy.wait_recv()
    fill_edges(edge_layers(edge_in2, corner_in2, 0), edge_layers(edge_in, corner_in, 2), False)
    for copy in layers2:
        copy.wait_recv()
    fill_rows(lambda at, c: (halo2[0, c, at, :], fresh[0, c, at, :], fresh[1, c, at, :], halo2[1, c, at, :]), k_rows, False)

    def put_packed(layer, c, start, new):
        packed[pl.ds(start, CHUNK), layer * 4 + c, :] = new

    sweep(lambda layer, at, c: fresh[layer, c, at, :], put_packed, False)

    pl.semaphore_wait(ready_sem, groups - 1)

    def pick(j):
        send[j] = packed[order_ref[0, j]]

    def target_group(i):
        return jnp.where(i % 2 == 1, groups // 2 - (i + 1) // 2, groups - groups // 2 + i // 2) % groups

    def spread(i, carry):
        other = (mine + target_group(i)) % groups
        for step in range(group):
            pick(other * group + step)
        for step in range(group):
            j = other * group + (place + step) % group
            remote(send.at[j], recv.at[me], spread_send_sem, spread_sem.at[mine], j, y).start()
        return carry

    lax.fori_loop(0, groups - 1, spread, 0)
    for step in range(group):
        pick(mine * group + step)
    for step in range(1, group):
        j = mine * group + (place + step) % group
        remote(send.at[j], recv.at[me], spread_send_sem, spread_sem.at[mine], j, y).start()
    pltpu.make_async_copy(send.at[me], recv.at[me], spread_sem.at[mine]).start()

    load_trial.wait()
    active = jnp.broadcast_to(active_ref[...], (8, LANES))
    upper = lax.broadcasted_iota(jnp.int32, (8, LANES), 0) < 4

    def creep(i, carry):
        g = (mine + groups - target_group(i)) % groups
        at = pl.ds(g * group, group)
        pltpu.make_async_copy(recv.at[at], recv.at[at], spread_sem.at[g]).wait()
        temp = recv[at]
        trial = trial_v[at]
        rate = CREEP_RATE * jnp.exp(-ACTIVATION / (temp + REFERENCE_TEMP))
        slip = jnp.zeros_like(trial)
        for newton in range(NEWTON):
            left = trial - slip
            pull = rate * (left * left)
            slip = slip - (slip - pull * left) / (1.0 + 3.0 * pull)
        sums = []
        for e in range(2):
            live = jnp.where(jnp.full((8, LANES), 2 * g + e, jnp.int32) < active, 1.0, 0.0)
            part = live * slip[4 * e : 4 * e + 4]
            stress_v[pl.ds(g * group + 4 * e, 4)] = trial[4 * e : 4 * e + 4] - part
            total = part[0] + part[1] + part[2] + part[3]
            sums.append((total + pltpu.roll(total, 4, 0)) * 0.125)
        strain_v[g] = jnp.where(upper, sums[0], sums[1])
        pltpu.make_async_copy(stress_v.at[at], stress_ref.at[at], out_sem.at[0]).start()
        return carry

    lax.fori_loop(0, groups, creep, 0)
    strain_copy = pltpu.make_async_copy(strain_v, strain_ref, out_sem.at[1])
    strain_copy.start()
    for copy in edges + layers + edges2 + layers2:
        copy.wait_send()
    most = pl.ds(0, n - 1)
    pltpu.make_async_copy(send.at[most], send.at[most], spread_send_sem).wait()
    pltpu.make_async_copy(stress_v, stress_ref, out_sem.at[0]).wait()
    strain_copy.wait()


def solution(mesh):
    slabs, sections, mechs = (mesh.shape[a] for a in ("slab", "iface", "mech"))
    n = slabs * mechs
    groups = n // (2 * mechs)

    def on_device(temp, cond, gap, partner, order, active, trial):
        depth, _, rows, radial = temp.shape
        f32 = jnp.float32
        any_space = pl.BlockSpec(memory_space=pl.ANY)
        vmem = pl.BlockSpec(memory_space=pltpu.VMEM)
        smem = pl.BlockSpec(memory_space=pltpu.SMEM)
        dma = pltpu.SemaphoreType.DMA
        stress, strain = pl.pallas_call(
            functools.partial(kernel, slabs, sections, mechs),
            out_shape=(
                jax.ShapeDtypeStruct((n, 8, LANES), f32),
                jax.ShapeDtypeStruct((groups, 8, LANES), f32),
            ),
            in_specs=[any_space, any_space, vmem, vmem, smem, vmem, any_space],
            out_specs=(any_space, any_space),
            scratch_shapes=[
                pltpu.VMEM((2, rows, radial), f32),
                pltpu.VMEM((2, rows, radial), f32),
                pltpu.VMEM((2, 2, rows, radial), f32),
                pltpu.VMEM((2, 4, rows, LANES), f32),
                pltpu.VMEM((2, 4, rows, LANES), f32),
                pltpu.VMEM((2, 3, 4, rows + 2 * PAD, LANES), f32),
                pltpu.VMEM((2, 4, rows, LANES), f32),
                pltpu.VMEM((2, 2, rows, LANES), f32),
                pltpu.VMEM((rows, LANES), f32),
                pltpu.VMEM((8, radial), f32),
                pltpu.VMEM((2 * rows, sections * rows), jnp.bfloat16),
                pltpu.VMEM((2, 8, radial), f32),
                pltpu.VMEM((3, 8, radial), f32),
                pltpu.VMEM((2, 2, 8, radial), f32),
                pltpu.VMEM((2, 8, radial), f32),
                pltpu.VMEM((3, 8, radial), f32),
                pltpu.VMEM((2, 2, 8, radial), f32),
                pltpu.VMEM((rows, 8, LANES), f32),
                pltpu.VMEM((n, 8, LANES), f32),
                pltpu.VMEM((n, 8, LANES), f32),
                pltpu.VMEM((n, 8, LANES), f32),
                pltpu.VMEM((n, 8, LANES), f32),
                pltpu.VMEM((groups, 8, LANES), f32),
                dma((3,)),
                dma((2,)),
                dma((20,)),
                dma((2, 2)),
                dma((3,)),
                dma((4,)),
                dma((2,)),
                dma((3,)),
                dma((4,)),
                dma,
                dma((groups,)),
                pltpu.SemaphoreType.REGULAR,
            ],
            compiler_params=pltpu.CompilerParams(
                collective_id=0, has_side_effects=True, vmem_limit_bytes=60 * 1024 * 1024
            ),
        )(
            temp.reshape(depth, rows, radial),
            cond.reshape(depth, rows, radial),
            gap.reshape(depth, rows),
            partner.reshape(1, rows),
            order,
            active,
            trial.reshape(n, 8, LANES),
        )
        return stress.reshape(trial.shape), strain.reshape(trial.shape[0] // 8, 1, 1, radial)

    placed = (
        P(("slab", "mech"), "iface", None, None),
        P(("slab", "mech"), "iface", None, None),
        P(("slab", "mech"), "iface", None),
        P("iface"),
        P("iface", None),
        P("iface", ("slab", "mech")),
        P(None, "iface", ("slab", "mech"), None),
    )
    return jax.shard_map(
        on_device,
        mesh=mesh,
        in_specs=placed,
        out_specs=(
            P(None, "iface", ("slab", "mech"), None),
            P(None, "iface", ("slab", "mech"), None),
        ),
        check_vma=False,
    )
```

time: 259 us -> 67.4 us (0.26)
  waiting for transfers between devices: 84.1 us -> 0 us
  Pallas kernels: 0 us -> 63.1 us
  starting transfers between devices: 57.6 us -> 0 us
  local copies, waits for them, and re-layouts: 43.3 us -> 2.86 us
  other arithmetic: 29.4 us -> 0 us
  blocking collectives: 23.5 us -> 0 us
  between operations: 15.6 us -> 1.29 us
  matrix products: 3.01 us -> 0 us
    pallas_call x0 -> x1, Pallas kernels: none -> 63.1 us  [on_device(): pl.pallas_call(functools.partial(kernel, slabs, sections, mechs), out_sha...]
    unnamed x4 -> x0, waiting for transfers between devices: 52.9 us -> none
    ppermute x12 -> x0, starting transfers between devices: 37.5 us -> none  [the longest x6 23.3 us: padded(): lax.ppermute(lax.slice_in_dim(block, block.shape[dim] - width, None, axis...]
    all_to_all x1 -> x0, waiting for transfers between devices: 30.2 us -> none  [on_device(): lax.all_to_all(permuted, ('slab', 'mech'), split_axis=1, concat_axis=0, t...]
    all_gather x2 -> x0, blocking collectives: 23.5 us -> none  [on_device(): compact_all = lax.all_gather(compact, 'iface', axis=1, tiled=True)]
    all_to_all x1 -> x0, starting transfers between devices: 20 us -> none  [on_device(): lax.all_to_all(permuted, ('slab', 'mech'), split_axis=1, concat_axis=0, t...]
    add x6 -> x0, other arithmetic: 13.2 us -> none  [the longest x2 10.5 us: on_device(): fresh = temp + conduction(padded_temp, padded_cond)]
    all_gather x2 -> x0, local copies, waits for them, and re-layouts: 7.95 us -> none  [on_device(): compact_all = lax.all_gather(compact, 'iface', axis=1, tiled=True)]
  transfers between devices with their start and end apart: 15 -> 0, of which waited for: 4 -> 0; matrix products, arithmetic and copies ran while one was open for 11% -> 0% of each run, Pallas kernels for 0% -> 0%
where the time goes in v1:
time: 67.4 us; the launch traced here: 67.2 us
  Pallas kernels  63.1 us (94%)
  local copies, waits for them, and re-layouts  2.86 us (4%)
  between operations  1.29 us (2%)
    pallas_call x1, Pallas kernels, on_device(): pl.pallas_call(functools.partial(kernel, slabs, sections, mechs), out_sha...  63.1 us
    unnamed x4, local copies, waits for them, and re-layouts  2.86 us

profile of v1, /device:TPU:1, one launch (start us, length us, event | category | flops | bytes accessed | tf_op | source)
XLA Modules:
  0.0 67.2 jit_solution(12901936744103960057)
XLA Ops:
  1.3 63.1 %shard_map.86 = (f32[128,8,128]{2,1,0:T(8,128)}, f32[16,8,128]{2,1,0:T(8,128)}) custom-call(f32[2,128,512]{2,1,0:T(8,128)} %bitcast.7, f32[2,128,512]{2,1,0:T(8,128)} %bitcast.8, f32[2,128]{1,0:T(2,128)} %bitcast.12, s32[1,128]{1,0:T(1,128)} %bitcast.13, s32[1,128]{1,0:T(1,128)} %order_ref.1, s32[1,1]{1,0:T(1,128)S(6)} %copy.13.active_ref, ...), custom_call_target="tpu_custom_call" | custom-call | tf_op jit(solution)/shard_map/pallas_call | solution.py:457
  64.3 0.0 copy-start
  64.3 2.2 %copy.14 = f32[256,1,1,512]{3,2,1,0:T(1,128)} copy(f32[256,1,1,512]{3,2,1,0:T(1,128)} %bitcast.10) | data formatting | bytes 1048576
  66.6 0.0 copy-done
  66.6 0.6 copy.15
Async XLA Ops:
  64.3 2.2 %copy-start = (f32[16,8,128]{2,1,0:T(8,128)S(1)}, f32[16,8,128]{2,1,0:T(8,128)}, u32[]{:S(2)}) copy-start(f32[16,8,128]{2,1,0:T(8,128)} %get-tuple-element.5) | copy-start | bytes 196612

commit v2 on v1

--- a/solution.py
+++ b/solution.py
@@ -24,13 +24,17 @@
     mechs,
     temp_ref,
     cond_ref,
+    gap_in,
+    partner_in,
+    order_in,
+    active_in,
+    trial_ref,
+    stress_ref,
+    strain_ref,
     gap_ref,
     partner_ref,
     order_ref,
     active_ref,
-    trial_ref,
-    stress_ref,
-    strain_ref,
     own_t,
     own_k,
     halo,
@@ -52,10 +56,7 @@
     send,
     recv,
     trial_v,
-    stress_v,
-    strain_v,
     load_sem,
-    out_sem,
     send_sem,
     layer_sem,
     edge_sem,
@@ -83,8 +84,12 @@
     load_t = pltpu.make_async_copy(temp_ref, own_t, load_sem.at[0])
     load_k = pltpu.make_async_copy(cond_ref, own_k, load_sem.at[1])
     load_trial = pltpu.make_async_copy(trial_ref, trial_v, load_sem.at[2])
-    load_t.start()
-    load_k.start()
+    load_gap = pltpu.make_async_copy(gap_in, gap_ref, load_sem.at[3])
+    load_partner = pltpu.make_async_copy(partner_in, partner_ref, load_sem.at[4])
+    load_order = pltpu.make_async_copy(order_in, order_ref, load_sem.at[5])
+    load_active = pltpu.make_async_copy(active_in, active_ref, load_sem.at[6])
+    for copy in (load_partner, load_gap, load_t, load_k, load_order, load_active):
+        copy.start()
 
     barrier = pltpu.get_barrier_semaphore()
 
@@ -99,7 +104,7 @@
         greet(k, section)
     for step in range(1, group):
         greet(mine * group + (place + step) % group, y)
-    for step in range(1, groups):
+    for step in (1, groups - 1):
         greet(((mine + step) % groups) * group + place, y)
 
     load_trial.start()
@@ -120,6 +125,8 @@
         shifted = index - base
         return jnp.where(shifted < 0.0, shifted + whole, shifted)
 
+    load_partner.wait()
+    load_gap.wait()
     partner_row = partner_ref[...].astype(jnp.float32)
     partner_column = as_column(relative(partner_row))
     cols[:, 0:1] = as_column(gap_ref[0:1, :])
@@ -146,12 +153,17 @@
         edge_out[e, 5:6, 3 * LANES : 4 * LANES] = zeros_row
         edge_out[e, 6:8, :] = jnp.zeros((2, 4 * LANES), jnp.float32)
         edge_out2[e] = jnp.zeros((8, 4 * LANES), jnp.float32)
-    pl.semaphore_wait(barrier, len(near) + group - 1 + groups - 1)
-
-    for step in range(1, groups):
-        pl.semaphore_signal(
-            ready_sem, inc=1, device_id=device(((mine + step) % groups) * group + place, y), device_id_type=MESH
-        )
+    pl.semaphore_wait(barrier, len(near) + group - 1 + 2)
+
+    def tell(level):
+        for step in sorted({2**level, groups - 2**level}):
+            other = ((mine + step) % groups) * group + place
+            pl.semaphore_signal(ready_sem.at[level], inc=1, device_id=device(other, y), device_id_type=MESH)
+
+    def hear(level):
+        pl.semaphore_wait(ready_sem.at[level], len({2**level, groups - 2**level}))
+
+    tell(0)
 
     def remote(source, target, sent, landed, k, section):
         return pltpu.make_async_remote_copy(
@@ -293,6 +305,8 @@
             addend[layer, 0] = jnp.where(lane_of == LANES - 1, -STEP * returned, 0.0)
             addend[layer, 1] = jnp.where(lane_of == 0, STEP * flux, 0.0)
 
+    hear(0)
+    tell(1)
     xbuf[6:8, :] = jnp.zeros((2, 4 * LANES), jnp.float32)
     for copy in edges[:3]:
         copy.wait_recv()
@@ -323,6 +337,8 @@
         return of
 
     fill_edges(edge_layers(edge_in, corner_in, 0), edge_layers(edge_in, corner_in, 2), True)
+    hear(1)
+    tell(2)
     for copy in layers:
         copy.wait_recv()
 
@@ -363,6 +379,9 @@
     for copy in edges2:
         copy.start()
 
+    hear(2)
+    tell(3)
+
     for copy in edges2[:3]:
         copy.wait_recv()
     found = gather(edge_out2, edge_in2, slots)
@@ -379,7 +398,8 @@
 
     sweep(lambda layer, at, c: fresh[layer, c, at, :], put_packed, False)
 
-    pl.semaphore_wait(ready_sem, groups - 1)
+    hear(3)
+    load_order.wait()
 
     def pick(j):
         send[j] = packed[order_ref[0, j]]
@@ -405,6 +425,7 @@
     pltpu.make_async_copy(send.at[me], recv.at[me], spread_sem.at[mine]).start()
 
     load_trial.wait()
+    load_active.wait()
     active = jnp.broadcast_to(active_ref[...], (8, LANES))
     upper = lax.broadcasted_iota(jnp.int32, (8, LANES), 0) < 4
 
@@ -424,22 +445,28 @@
         for e in range(2):
             live = jnp.where(jnp.full((8, LANES), 2 * g + e, jnp.int32) < active, 1.0, 0.0)
             part = live * slip[4 * e : 4 * e + 4]
-            stress_v[pl.ds(g * group + 4 * e, 4)] = trial[4 * e : 4 * e + 4] - part
+            stress_ref[pl.ds(g * group + 4 * e, 4)] = trial[4 * e : 4 * e + 4] - part
             total = part[0] + part[1] + part[2] + part[3]
             sums.append((total + pltpu.roll(total, 4, 0)) * 0.125)
-        strain_v[g] = jnp.where(upper, sums[0], sums[1])
-        pltpu.make_async_copy(stress_v.at[at], stress_ref.at[at], out_sem.at[0]).start()
+        strain_ref[g] = jnp.where(upper, sums[0], sums[1])
         return carry
 
     lax.fori_loop(0, groups, creep, 0)
-    strain_copy = pltpu.make_async_copy(strain_v, strain_ref, out_sem.at[1])
-    strain_copy.start()
     for copy in edges + layers + edges2 + layers2:
         copy.wait_send()
     most = pl.ds(0, n - 1)
     pltpu.make_async_copy(send.at[most], send.at[most], spread_send_sem).wait()
-    pltpu.make_async_copy(stress_v, stress_ref, out_sem.at[0]).wait()
-    strain_copy.wait()
+
+
+def hand_over(stress_ref, strain_ref, stress_out, strain_out, sem):
+    copies = [
+        pltpu.make_async_copy(stress_ref, stress_out, sem.at[0]),
+        pltpu.make_async_copy(strain_ref, strain_out, sem.at[1]),
+    ]
+    for copy in copies:
+        copy.start()
+    for copy in copies:
+        copy.wait()
 
 
 def solution(mesh):
@@ -451,8 +478,8 @@
         depth, _, rows, radial = temp.shape
         f32 = jnp.float32
         any_space = pl.BlockSpec(memory_space=pl.ANY)
+        hbm = pl.BlockSpec(memory_space=pltpu.HBM)
         vmem = pl.BlockSpec(memory_space=pltpu.VMEM)
-        smem = pl.BlockSpec(memory_space=pltpu.SMEM)
         dma = pltpu.SemaphoreType.DMA
         stress, strain = pl.pallas_call(
             functools.partial(kernel, slabs, sections, mechs),
@@ -460,9 +487,13 @@
                 jax.ShapeDtypeStruct((n, 8, LANES), f32),
                 jax.ShapeDtypeStruct((groups, 8, LANES), f32),
             ),
-            in_specs=[any_space, any_space, vmem, vmem, smem, vmem, any_space],
-            out_specs=(any_space, any_space),
+            in_specs=[hbm] * 7,
+            out_specs=(vmem, vmem),
             scratch_shapes=[
+                pltpu.VMEM((depth, rows), f32),
+                pltpu.VMEM((1, rows), jnp.int32),
+                pltpu.SMEM((1, rows), jnp.int32),
+                pltpu.VMEM((1, 1), jnp.int32),
                 pltpu.VMEM((2, rows, radial), f32),
                 pltpu.VMEM((2, rows, radial), f32),
                 pltpu.VMEM((2, 2, rows, radial), f32),
@@ -484,10 +515,7 @@
                 pltpu.VMEM((n, 8, LANES), f32),
                 pltpu.VMEM((n, 8, LANES), f32),
                 pltpu.VMEM((n, 8, LANES), f32),
-                pltpu.VMEM((n, 8, LANES), f32),
-                pltpu.VMEM((groups, 8, LANES), f32),
-                dma((3,)),
-                dma((2,)),
+                dma((7,)),
                 dma((20,)),
                 dma((2, 2)),
                 dma((3,)),
@@ -497,20 +525,36 @@
                 dma((4,)),
                 dma,
                 dma((groups,)),
-                pltpu.SemaphoreType.REGULAR,
+                pltpu.SemaphoreType.REGULAR((4,)),
             ],
             compiler_params=pltpu.CompilerParams(
-                collective_id=0, has_side_effects=True, vmem_limit_bytes=60 * 1024 * 1024
+                collective_id=0, has_side_effects=True, vmem_limit_bytes=48 * 1024 * 1024
             ),
         )(
-            temp.reshape(depth, rows, radial),
-            cond.reshape(depth, rows, radial),
-            gap.reshape(depth, rows),
-            partner.reshape(1, rows),
-            order,
-            active,
-            trial.reshape(n, 8, LANES),
+            *[
+                x if x is active else pltpu.with_memory_space_constraint(x, pltpu.HBM)
+                for x in (
+                    temp.reshape(depth, rows, radial),
+                    cond.reshape(depth, rows, radial),
+                    gap.reshape(depth, rows),
+                    partner.reshape(1, rows),
+                    order,
+                    active,
+                    trial.reshape(n, 8, LANES),
+                )
+            ]
         )
+        stress, strain = pl.pallas_call(
+            hand_over,
+            out_shape=(
+                jax.ShapeDtypeStruct((n, 8, LANES), f32),
+                jax.ShapeDtypeStruct((groups, 8, LANES), f32),
+            ),
+            in_specs=[vmem, vmem],
+            out_specs=(any_space, any_space),
+            scratch_shapes=[dma((2,))],
+            compiler_params=pltpu.CompilerParams(vmem_limit_bytes=8 * 1024 * 1024),
+        )(stress, strain)
         return stress.reshape(trial.shape), strain.reshape(trial.shape[0] // 8, 1, 1, radial)
 
     placed = (

time: 67.4 us -> 60.2 us (0.89)
  Pallas kernels: 63.1 us -> 58.8 us
  local copies, waits for them, and re-layouts: 2.86 us -> 0 us
    pallas_call x1, Pallas kernels: 63.1 us -> 58 us  [on_device(): pl.pallas_call(functools.partial(kernel, slabs, sections, mechs), out_sha...]
    unnamed x4 -> x0, local copies, waits for them, and re-layouts: 2.86 us -> none
    pallas_call x0 -> x1, Pallas kernels: none -> 0.82 us  [on_device(): pl.pallas_call(hand_over, out_shape=(jax.ShapeDtypeStruct((n, 8, LANES),...]
where the time goes in v2:
time: 60.2 us; the launch traced here: 60.1 us
  Pallas kernels  58.8 us (98%)
  between operations  1.29 us (2%)
    pallas_call x1, Pallas kernels, on_device(): pl.pallas_call(functools.partial(kernel, slabs, sections, mechs), out_sha...  58 us

profile of v2, /device:TPU:1, one launch (start us, length us, event | category | flops | bytes accessed | tf_op | source)
XLA Modules:
  0.0 60.1 jit_solution(18222832210444501065)
XLA Ops:
  1.3 58.0 %shard_map.86 = (f32[128,8,128]{2,1,0:T(8,128)S(1)}, f32[16,8,128]{2,1,0:T(8,128)S(1)}) custom-call(f32[2,128,512]{2,1,0:T(8,128)} %bitcast.7, f32[2,128,512]{2,1,0:T(8,128)} %bitcast.8, f32[2,128]{1,0:T(2,128)} %bitcast.10, s32[1,128]{1,0:T(1,128)} %bitcast.11, s32[1,128]{1,0:T(1,128)} %order_in.1, s32[1,1]{1,0:T(1,128)S(6)} %copy.11.active_in, ...), custom_call_target="tpu_custom_call" | custom-call | tf_op jit(solution)/shard_map/pallas_call | solution.py:484
  59.2 0.8 %shard_map.87 = (f32[128,8,128]{2,1,0:T(8,128)}, f32[16,8,128]{2,1,0:T(8,128)}) custom-call(f32[128,8,128]{2,1,0:T(8,128)S(1)} %get-tuple-element.6.stress_ref, f32[16,8,128]{2,1,0:T(8,128)S(1)} %get-tuple-element.7.strain_ref), custom_call_target="tpu_custom_call" | custom-call | tf_op jit(solution)/shard_map/pallas_call | solution.py:547

commit v3 on v2

--- a/solution.py
+++ b/solution.py
@@ -16,6 +16,8 @@
 LANES = 128
 PAD = 8
 CHUNK = 32
+EARLY = 2
+FAR = 5
 
 
 def kernel(
@@ -49,9 +51,12 @@
     edge_out,
     edge_in,
     corner_in,
-    edge_out2,
-    edge_in2,
-    corner_in2,
+    outer_out,
+    outer_in,
+    outer_corner,
+    inner_out,
+    inner_in,
+    inner_corner,
     packed,
     send,
     recv,
@@ -62,8 +67,10 @@
     edge_sem,
     corner_sem,
     layer2_sem,
-    edge2_sem,
-    corner2_sem,
+    outer_sem,
+    outer_corner_sem,
+    inner_sem,
+    inner_corner_sem,
     spread_send_sem,
     spread_sem,
     ready_sem,
@@ -152,7 +159,8 @@
         edge_out[e, 5:6, 2 * LANES : 3 * LANES] = partner_row
         edge_out[e, 5:6, 3 * LANES : 4 * LANES] = zeros_row
         edge_out[e, 6:8, :] = jnp.zeros((2, 4 * LANES), jnp.float32)
-        edge_out2[e] = jnp.zeros((8, 4 * LANES), jnp.float32)
+        outer_out[e] = jnp.zeros((8, 2 * LANES), jnp.float32)
+        inner_out[e] = jnp.zeros((8, 2 * LANES), jnp.float32)
     pl.semaphore_wait(barrier, len(near) + group - 1 + 2)
 
     def tell(level):
@@ -171,11 +179,12 @@
             device_id=device(k, section), device_id_type=MESH,
         )
 
-    def edge_copies(out, into, corners, edge_landed, corner_landed, first):
+    def edge_copies(out, into, corners, edge_landed, corner_landed, first, faces=True):
+        across = [remote(out.at[0], into.at[2], send_sem.at[first + 2], edge_landed.at[2], me, y_far)] if faces else []
         return [
             remote(out.at[1], into.at[0], send_sem.at[first], edge_landed.at[0], me, y_high),
             remote(out.at[0], into.at[1], send_sem.at[first + 1], edge_landed.at[1], me, y_low),
-            remote(out.at[0], into.at[2], send_sem.at[first + 2], edge_landed.at[2], me, y_far),
+            *across,
             remote(out.at[1], corners.at[0, 0], send_sem.at[first + 3], corner_landed.at[0], above, y_high),
             remote(out.at[0], corners.at[0, 1], send_sem.at[first + 4], corner_landed.at[1], above, y_low),
             remote(out.at[1], corners.at[1, 0], send_sem.at[first + 5], corner_landed.at[2], below, y_high),
@@ -185,13 +194,24 @@
     edges = edge_copies(edge_out, edge_in, corner_in, edge_sem, corner_sem, 0)
     for copy in edges:
         copy.start()
-    layers = [
-        remote(temp_ref.at[0], halo.at[1, 0], send_sem.at[7], layer_sem.at[1, 0], below, y),
-        remote(temp_ref.at[1], halo.at[0, 0], send_sem.at[8], layer_sem.at[0, 0], above, y),
-        remote(cond_ref.at[0], halo.at[1, 1], send_sem.at[9], layer_sem.at[1, 1], below, y),
-        remote(cond_ref.at[1], halo.at[0, 1], send_sem.at[10], layer_sem.at[0, 1], above, y),
-    ]
-    for copy in layers:
+
+    def half_of(half):
+        return pl.ds(2 * half * LANES, 2 * LANES)
+
+    def layer_copies(half):
+        out = []
+        for f, ref in enumerate((temp_ref, cond_ref)):
+            for side, (layer, k) in enumerate(((1, above), (0, below))):
+                out.append(
+                    remote(
+                        ref.at[layer, :, half_of(half)], halo.at[side, f, :, half_of(half)],
+                        send_sem.at[7 + 4 * half + 2 * f + side], layer_sem.at[side, f, half], k, y,
+                    )
+                )
+        return out
+
+    layers = [layer_copies(0), layer_copies(1)]
+    for copy in layers[0]:
         copy.start()
 
     has_below = jnp.where(me > 0, 0.5, 0.0).astype(jnp.float32)
@@ -205,7 +225,7 @@
             second + 0.5 * first + has_above * after,
         )
 
-    def fill_edges(t_of, k_of, with_cond):
+    def fill_edges(t_of, k_of, with_cond, half):
         for e, row, there in ((0, PAD - 1, has_low), (1, PAD + rows, has_high)):
             ts, ks = t_of(e), k_of(e)
             sums = [across_layers(*ts), across_layers(*[a * b for a, b in zip(ts, ks)])]
@@ -214,15 +234,15 @@
             for f, pair in enumerate(sums):
                 for layer in range(2):
                     edge = there * pair[layer]
-                    for c in range(4):
-                        u[layer, f, c, row : row + 1, :] = edge[:, c * LANES : (c + 1) * LANES]
-
-    def fill_rows(t_of, k_of, with_cond):
+                    for j in range(2):
+                        u[layer, f, 2 * half + j, row : row + 1, :] = edge[:, j * LANES : (j + 1) * LANES]
+
+    def fill_rows(t_of, k_of, with_cond, half):
         def body(i, carry):
             start = pl.multiple_of(i * CHUNK, CHUNK)
             at = pl.ds(start, CHUNK)
             to = pl.ds(pl.multiple_of(start + PAD, 8), CHUNK)
-            for c in range(4):
+            for c in (2 * half, 2 * half + 1):
                 ts, ks = t_of(at, c), k_of(at, c)
                 sums = [across_layers(*ts), across_layers(*[a * b for a, b in zip(ts, ks)])]
                 if with_cond:
@@ -251,42 +271,37 @@
             v[1] + 0.5 * (jnp.where(first_lane, right[0], right[1]) + jnp.where(last_lane, 0.0, left[1])),
         ]
 
-    def sweep(t_of, put, first):
+    def sweep(t_of, put, first, half, faces):
         for layer in range(2):
-            for half in range(2):
-                for i in range(rows // CHUNK):
-                    start = i * CHUNK
-                    at = pl.ds(start, CHUNK)
-                    spread_t = spread_of(layer, 0, 2 * half, start)
-                    spread_kt = spread_of(layer, 1, 2 * half, start)
-                    spread_k = spread_of(layer, 2, 2 * half, start) if first else None
-                    for j in range(2):
-                        c = 2 * half + j
-                        k = own_k[layer, at, c * LANES : (c + 1) * LANES]
-                        t = t_of(layer, at, c)
-                        if first:
-                            weight = jnp.full((CHUNK, LANES), 8.0, jnp.float32)
-                            if c == 1:
-                                weight = jnp.where(last_lane, 6.0, weight)
-                            if c == 2:
-                                weight = jnp.where(first_lane, 6.0, weight)
-                            drain = weight * k + spread_k[j]
-                            keep[layer, c, at, :] = drain
-                        else:
-                            drain = keep[layer, c, at, :]
-                        new = t + STEP * (k * spread_t[j] + spread_kt[j] - t * drain)
-                        if c in (1, 2):
-                            new = new + addend[layer, c - 1, at, :]
-                        put(layer, c, start, new)
-
-    def gather(faces, into, slots):
-        for q, block in enumerate([faces[0], *[into[s] for s in slots]]):
-            for layer in range(4):
-                xbuf[layer : layer + 1, q * LANES : (q + 1) * LANES] = block[4:5, layer * LANES : (layer + 1) * LANES]
-            for layer in range(2):
-                xbuf[4 + layer : 5 + layer, q * LANES : (q + 1) * LANES] = block[
-                    5:6, layer * LANES : (layer + 1) * LANES
-                ]
+            for i in range(rows // CHUNK):
+                start = i * CHUNK
+                at = pl.ds(start, CHUNK)
+                spread_t = spread_of(layer, 0, 2 * half, start)
+                spread_kt = spread_of(layer, 1, 2 * half, start)
+                spread_k = spread_of(layer, 2, 2 * half, start) if first else None
+                for j in range(2):
+                    c = 2 * half + j
+                    k = own_k[layer, at, c * LANES : (c + 1) * LANES]
+                    t = t_of(layer, at, c)
+                    if first:
+                        weight = jnp.full((CHUNK, LANES), 8.0, jnp.float32)
+                        if c == 1:
+                            weight = jnp.where(last_lane, 6.0, weight)
+                        if c == 2:
+                            weight = jnp.where(first_lane, 6.0, weight)
+                        drain = weight * k + spread_k[j]
+                        keep[layer, c, at, :] = drain
+                    else:
+                        drain = keep[layer, c, at, :]
+                    new = t + STEP * (k * spread_t[j] + spread_kt[j] - t * drain)
+                    if c in faces:
+                        new = new + addend[layer, c - 1, at, :]
+                    put(layer, c, start, new)
+
+    def gather(rows_of, slots):
+        for q, slot in enumerate((None, *slots)):
+            for i, row in enumerate(rows_of(slot)):
+                xbuf[i : i + 1, q * LANES : (q + 1) * LANES] = row
         x = xbuf[...]
         high = x.astype(jnp.bfloat16)
         rest = x - high.astype(jnp.float32)
@@ -311,129 +326,204 @@
     for copy in edges[:3]:
         copy.wait_recv()
     slots = (1, 2, 0)
-    for q, block in enumerate([edge_out[0], *[edge_in[s] for s in slots]]):
-        theirs = relative(block[5:6, 2 * LANES : 3 * LANES])
+
+    def start_rows(slot):
+        tile = edge_out[0] if slot is None else edge_in[slot]
+        return [tile[4:5, i * LANES : (i + 1) * LANES] for i in range(4)] + [
+            tile[5:6, i * LANES : (i + 1) * LANES] for i in range(2)
+        ]
+
+    for q, tile in enumerate([edge_out[0], *[edge_in[slot] for slot in slots]]):
+        theirs = relative(tile[5:6, 2 * LANES : 3 * LANES])
         hot[rows : 2 * rows, q * LANES : (q + 1) * LANES] = jnp.where(
             row_of.astype(jnp.float32) == theirs, 1.0, 0.0
         ).astype(jnp.bfloat16)
-    found = gather(edge_out, edge_in, slots)
+    found = gather(start_rows, slots)
     cols[:, 2:4] = found[rows : 2 * rows, 4:6]
     gap_flux(
         found,
         lambda layer: (own_t[layer, :, 2 * LANES - 1 : 2 * LANES], own_t[layer, :, 2 * LANES : 2 * LANES + 1]),
     )
+    for copy in layers[1]:
+        copy.start()
     for copy in edges[3:]:
         copy.wait_recv()
 
-    def edge_layers(into, corners, row):
+    def edge_layers(into, corners, row, columns):
         def of(e):
             return (
-                corners[0, e, row + 1 : row + 2, :],
-                into[e, row : row + 1, :],
-                into[e, row + 1 : row + 2, :],
-                corners[1, e, row : row + 1, :],
+                corners[0, e, row + 1 : row + 2, columns],
+                into[e, row : row + 1, columns],
+                into[e, row + 1 : row + 2, columns],
+                corners[1, e, row : row + 1, columns],
             )
 
         return of
 
-    fill_edges(edge_layers(edge_in, corner_in, 0), edge_layers(edge_in, corner_in, 2), True)
+    def half_slice(half):
+        return slice(2 * half * LANES, 2 * (half + 1) * LANES)
+
+    def block(c):
+        return slice(c * LANES, (c + 1) * LANES)
+
+    def k_rows(at, c):
+        return (halo[0, 1, at, block(c)], own_k[0, at, block(c)], own_k[1, at, block(c)], halo[1, 1, at, block(c)])
+
+    def t_rows(at, c):
+        return (halo[0, 0, at, block(c)], own_t[0, at, block(c)], own_t[1, at, block(c)], halo[1, 0, at, block(c)])
+
+    def put_fresh(layer, c, start, new):
+        fresh[layer, c, pl.ds(start, CHUNK), :] = new
+
+    def first_sweep(half):
+        columns = half_slice(half)
+        fill_edges(
+            edge_layers(edge_in, corner_in, 0, columns), edge_layers(edge_in, corner_in, 2, columns), True, half
+        )
+        for copy in layers[half]:
+            copy.wait_recv()
+        fill_rows(t_rows, k_rows, True, half)
+        sweep(lambda layer, at, c: own_t[layer, at, block(c)], put_fresh, True, half, (1, 2))
+
+    def fresh_copies(half):
+        pair = pl.ds(2 * half, 2)
+        return [
+            remote(fresh.at[1, pair], halo2.at[0, pair], send_sem.at[15 + 2 * half], layer2_sem.at[0, half], above, y),
+            remote(fresh.at[0, pair], halo2.at[1, pair], send_sem.at[16 + 2 * half], layer2_sem.at[1, half], below, y),
+        ]
+
+    def fresh_edges(out, half):
+        for e, at in ((0, 0), (1, rows - 1)):
+            for layer in range(2):
+                for j in range(2):
+                    out[e, layer : layer + 1, block(j)] = fresh[layer, 2 * half + j, at : at + 1, :]
+
     hear(1)
     tell(2)
-    for copy in layers:
-        copy.wait_recv()
-
-    def block(c):
-        return slice(c * LANES, (c + 1) * LANES)
-
-    def k_rows(at, c):
-        return (halo[0, 1, at, block(c)], own_k[0, at, block(c)], own_k[1, at, block(c)], halo[1, 1, at, block(c)])
-
-    fill_rows(
-        lambda at, c: (halo[0, 0, at, block(c)], own_t[0, at, block(c)], own_t[1, at, block(c)], halo[1, 0, at, block(c)]),
-        k_rows,
-        True,
-    )
-
-    def put_fresh(layer, c, start, new):
-        fresh[layer, c, pl.ds(start, CHUNK), :] = new
-
-    sweep(lambda layer, at, c: own_t[layer, at, block(c)], put_fresh, True)
-
-    layers2 = [
-        remote(fresh.at[0], halo2.at[1], send_sem.at[18], layer2_sem.at[1], below, y),
-        remote(fresh.at[1], halo2.at[0], send_sem.at[19], layer2_sem.at[0], above, y),
-    ]
-    for copy in layers2:
-        copy.start()
-    for e, at in ((0, 0), (1, rows - 1)):
-        for layer in range(2):
-            for c in range(4):
-                edge_out2[e, layer : layer + 1, block(c)] = fresh[layer, c, at : at + 1, :]
+    first_sweep(0)
+    layers2 = [fresh_copies(0), fresh_copies(1)]
+    for copy in layers2[0]:
+        copy.start()
+    fresh_edges(outer_out, 0)
+    outer = edge_copies(outer_out, outer_in, outer_corner, outer_sem, outer_corner_sem, 19, faces=False)
+    for copy in outer:
+        copy.start()
+    hear(2)
+    tell(3)
+    first_sweep(1)
     for layer in range(2):
         compact = as_row(fresh[layer, 1, :, LANES - 1 : LANES])
         canister = as_row(fresh[layer, 2, :, 0:1])
         for e in range(2):
-            edge_out2[e, 4:5, layer * LANES : (layer + 1) * LANES] = compact
-            edge_out2[e, 4:5, (2 + layer) * LANES : (3 + layer) * LANES] = canister
-    edges2 = edge_copies(edge_out2, edge_in2, corner_in2, edge2_sem, corner2_sem, 11)
-    for copy in edges2:
-        copy.start()
-
-    hear(2)
-    tell(3)
-
-    for copy in edges2[:3]:
+            inner_out[e, 4:5, block(layer)] = compact
+            inner_out[e, 5:6, block(layer)] = canister
+    fresh_edges(inner_out, 1)
+    inner = edge_copies(inner_out, inner_in, inner_corner, inner_sem, inner_corner_sem, 26)
+    for copy in inner:
+        copy.start()
+    for copy in layers2[1]:
+        copy.start()
+
+    def put_packed(layer, c, start, new):
+        packed[pl.ds(start, CHUNK), 2 * c + layer, :] = new
+
+    def second_sweep(half, into, corners, faces):
+        fill_edges(
+            edge_layers(into, corners, 0, slice(0, 2 * LANES)),
+            edge_layers(edge_in, corner_in, 2, half_slice(half)),
+            False,
+            half,
+        )
+        for copy in layers2[half]:
+            copy.wait_recv()
+        fill_rows(
+            lambda at, c: (halo2[0, c, at, :], fresh[0, c, at, :], fresh[1, c, at, :], halo2[1, c, at, :]),
+            k_rows,
+            False,
+            half,
+        )
+        sweep(lambda layer, at, c: fresh[layer, c, at, :], put_packed, False, half, faces)
+
+    for copy in outer:
         copy.wait_recv()
-    found = gather(edge_out2, edge_in2, slots)
-    gap_flux(found, lambda layer: (fresh[layer, 1, :, LANES - 1 : LANES], fresh[layer, 2, :, 0:1]))
-    for copy in edges2[3:]:
-        copy.wait_recv()
-    fill_edges(edge_layers(edge_in2, corner_in2, 0), edge_layers(edge_in, corner_in, 2), False)
-    for copy in layers2:
-        copy.wait_recv()
-    fill_rows(lambda at, c: (halo2[0, c, at, :], fresh[0, c, at, :], fresh[1, c, at, :], halo2[1, c, at, :]), k_rows, False)
-
-    def put_packed(layer, c, start, new):
-        packed[pl.ds(start, CHUNK), layer * 4 + c, :] = new
-
-    sweep(lambda layer, at, c: fresh[layer, c, at, :], put_packed, False)
+    second_sweep(0, outer_in, outer_corner, ())
 
     hear(3)
     load_order.wait()
 
-    def pick(j):
-        send[j] = packed[order_ref[0, j]]
-
     def target_group(i):
         return jnp.where(i % 2 == 1, groups // 2 - (i + 1) // 2, groups - groups // 2 + i // 2) % groups
 
-    def spread(i, carry):
-        other = (mine + target_group(i)) % groups
-        for step in range(group):
-            pick(other * group + step)
-        for step in range(group):
-            j = other * group + (place + step) % group
-            remote(send.at[j], recv.at[me], spread_send_sem, spread_sem.at[mine], j, y).start()
-        return carry
-
-    lax.fori_loop(0, groups - 1, spread, 0)
+    def pick(j, first, count):
+        send[j, first : first + count] = packed[order_ref[0, j], first : first + count]
+
+    def post(j, first, count, part):
+        span = pl.ds(first, count)
+        remote(
+            send.at[j, span], recv.at[me, span], spread_send_sem.at[part], spread_sem.at[part, mine], j, y
+        ).start()
+
+    def spread(begin, end, first, count, part):
+        def body(i, carry):
+            other = (mine + target_group(i)) % groups
+            for step in range(group):
+                pick(other * group + step, first, count)
+            for step in range(group):
+                post(other * group + (place + step) % group, first, count, part)
+            return carry
+
+        lax.fori_loop(begin, end, body, 0)
+
+    spread(0, FAR, 0, EARLY, 0)
+
+    for copy in inner[:3]:
+        copy.wait_recv()
+
+    def fresh_rows(slot):
+        tile = inner_out[0] if slot is None else inner_in[slot]
+        return [tile[row : row + 1, block(layer)] for row in (4, 5) for layer in range(2)]
+
+    found = gather(fresh_rows, slots)
+    gap_flux(found, lambda layer: (fresh[layer, 1, :, LANES - 1 : LANES], fresh[layer, 2, :, 0:1]))
+    for layer in range(2):
+        packed[:, 2 + layer, :] = packed[:, 2 + layer, :] + addend[layer, 0]
+    for copy in inner[3:]:
+        copy.wait_recv()
+    second_sweep(1, inner_in, inner_corner, (2,))
+    spread(0, FAR, EARLY, 8 - EARLY, 1)
+    spread(FAR, groups - 1, 0, 8, 2)
     for step in range(group):
-        pick(mine * group + step)
+        pick(mine * group + step, 0, 8)
     for step in range(1, group):
-        j = mine * group + (place + step) % group
-        remote(send.at[j], recv.at[me], spread_send_sem, spread_sem.at[mine], j, y).start()
-    pltpu.make_async_copy(send.at[me], recv.at[me], spread_sem.at[mine]).start()
+        post(mine * group + (place + step) % group, 0, 8, 2)
+    pltpu.make_async_copy(send.at[me], recv.at[me], spread_sem.at[2, mine]).start()
 
     load_trial.wait()
     load_active.wait()
     active = jnp.broadcast_to(active_ref[...], (8, LANES))
+    sublane = lax.broadcasted_iota(jnp.int32, (8, LANES), 0)
+    in_order = jnp.where(sublane < 4, 2 * sublane, 2 * sublane - 7)
     upper = lax.broadcasted_iota(jnp.int32, (8, LANES), 0) < 4
 
-    def creep(i, carry):
-        g = (mine + groups - target_group(i)) % groups
+    def source(i):
+        return (mine + groups - target_group(i)) % groups
+
+    def creep_far(i, carry):
+        g = source(i)
         at = pl.ds(g * group, group)
-        pltpu.make_async_copy(recv.at[at], recv.at[at], spread_sem.at[g]).wait()
-        temp = recv[at]
+        for part, span in enumerate((pl.ds(0, EARLY), pl.ds(EARLY, 8 - EARLY))):
+            pltpu.make_async_copy(recv.at[at, span], recv.at[at, span], spread_sem.at[part, g]).wait()
+        return creep(g, carry)
+
+    def creep_near(i, carry):
+        g = source(i)
+        at = pl.ds(g * group, group)
+        pltpu.make_async_copy(recv.at[at], recv.at[at], spread_sem.at[2, g]).wait()
+        return creep(g, carry)
+
+    def creep(g, carry):
+        at = pl.ds(g * group, group)
+        temp = jnp.stack([jnp.take_along_axis(recv[g * group + i], in_order, axis=0) for i in range(group)])
         trial = trial_v[at]
         rate = CREEP_RATE * jnp.exp(-ACTIVATION / (temp + REFERENCE_TEMP))
         slip = jnp.zeros_like(trial)
@@ -451,11 +541,15 @@
         strain_ref[g] = jnp.where(upper, sums[0], sums[1])
         return carry
 
-    lax.fori_loop(0, groups, creep, 0)
-    for copy in edges + layers + edges2 + layers2:
+    lax.fori_loop(0, FAR, creep_far, 0)
+    lax.fori_loop(FAR, groups, creep_near, 0)
+    for copy in edges + layers[0] + layers[1] + outer + inner + layers2[0] + layers2[1]:
         copy.wait_send()
-    most = pl.ds(0, n - 1)
-    pltpu.make_async_copy(send.at[most], send.at[most], spread_send_sem).wait()
+    far, near_by = pl.ds(0, FAR * group), pl.ds(0, n - 1 - FAR * group)
+    for part, sent in enumerate(
+        (send.at[far, pl.ds(0, EARLY)], send.at[far, pl.ds(EARLY, 8 - EARLY)], send.at[near_by])
+    ):
+        pltpu.make_async_copy(sent, sent, spread_send_sem.at[part]).wait()
 
 
 def hand_over(stress_ref, strain_ref, stress_out, strain_out, sem):
@@ -508,23 +602,28 @@
                 pltpu.VMEM((2, 8, radial), f32),
                 pltpu.VMEM((3, 8, radial), f32),
                 pltpu.VMEM((2, 2, 8, radial), f32),
-                pltpu.VMEM((2, 8, radial), f32),
-                pltpu.VMEM((3, 8, radial), f32),
-                pltpu.VMEM((2, 2, 8, radial), f32),
+                pltpu.VMEM((2, 8, radial // 2), f32),
+                pltpu.VMEM((3, 8, radial // 2), f32),
+                pltpu.VMEM((2, 2, 8, radial // 2), f32),
+                pltpu.VMEM((2, 8, radial // 2), f32),
+                pltpu.VMEM((3, 8, radial // 2), f32),
+                pltpu.VMEM((2, 2, 8, radial // 2), f32),
                 pltpu.VMEM((rows, 8, LANES), f32),
                 pltpu.VMEM((n, 8, LANES), f32),
                 pltpu.VMEM((n, 8, LANES), f32),
                 pltpu.VMEM((n, 8, LANES), f32),
                 dma((7,)),
-                dma((20,)),
+                dma((33,)),
+                dma((2, 2, 2)),
+                dma((3,)),
+                dma((4,)),
                 dma((2, 2)),
                 dma((3,)),
                 dma((4,)),
-                dma((2,)),
                 dma((3,)),
                 dma((4,)),
-                dma,
-                dma((groups,)),
+                dma((3,)),
+                dma((3, groups)),
                 pltpu.SemaphoreType.REGULAR((4,)),
             ],
             compiler_params=pltpu.CompilerParams(

time: 60.2 us -> 58.6 us (0.973)
  Pallas kernels: 58.8 us -> 57.2 us
    pallas_call x1, Pallas kernels: 58 us -> 56.4 us  [on_device(): pl.pallas_call(functools.partial(kernel, slabs, sections, mechs), out_sha...]
where the time goes in v3:
time: 58.6 us; the launch traced here: 58.5 us
  Pallas kernels  57.2 us (98%)
  between operations  1.29 us (2%)
    pallas_call x1, Pallas kernels, on_device(): pl.pallas_call(functools.partial(kernel, slabs, sections, mechs), out_sha...  56.4 us

profile of v3, /device:TPU:1, one launch (start us, length us, event | category | flops | bytes accessed | tf_op | source)
XLA Modules:
  0.0 58.5 jit_solution(14907536790573567695)
XLA Ops:
  1.3 56.4 %shard_map.86 = (f32[128,8,128]{2,1,0:T(8,128)S(1)}, f32[16,8,128]{2,1,0:T(8,128)S(1)}) custom-call(f32[2,128,512]{2,1,0:T(8,128)} %bitcast.7, f32[2,128,512]{2,1,0:T(8,128)} %bitcast.8, f32[2,128]{1,0:T(2,128)} %bitcast.10, s32[1,128]{1,0:T(1,128)} %bitcast.11, s32[1,128]{1,0:T(1,128)} %order_in.1, s32[1,1]{1,0:T(1,128)S(6)} %copy.11.active_in, ...), custom_call_target="tpu_custom_call" | custom-call | tf_op jit(solution)/shard_map/pallas_call | solution.py:578
  57.6 0.8 %shard_map.87 = (f32[128,8,128]{2,1,0:T(8,128)}, f32[16,8,128]{2,1,0:T(8,128)}) custom-call(f32[128,8,128]{2,1,0:T(8,128)S(1)} %get-tuple-element.6.stress_ref, f32[16,8,128]{2,1,0:T(8,128)S(1)} %get-tuple-element.7.strain_ref), custom_call_target="tpu_custom_call" | custom-call | tf_op jit(solution)/shard_map/pallas_call | solution.py:646

commit v4 on v3

--- a/solution.py
+++ b/solution.py
@@ -211,7 +211,7 @@
         return out
 
     layers = [layer_copies(0), layer_copies(1)]
-    for copy in layers[0]:
+    for copy in layers[0] + layers[1]:
         copy.start()
 
     has_below = jnp.where(me > 0, 0.5, 0.0).astype(jnp.float32)
@@ -325,6 +325,8 @@
     xbuf[6:8, :] = jnp.zeros((2, 4 * LANES), jnp.float32)
     for copy in edges[:3]:
         copy.wait_recv()
+    hear(1)
+    tell(2)
     slots = (1, 2, 0)
 
     def start_rows(slot):
@@ -344,8 +346,8 @@
         found,
         lambda layer: (own_t[layer, :, 2 * LANES - 1 : 2 * LANES], own_t[layer, :, 2 * LANES : 2 * LANES + 1]),
     )
-    for copy in layers[1]:
-        copy.start()
+    hear(2)
+    tell(3)
     for copy in edges[3:]:
         copy.wait_recv()
 
@@ -398,8 +400,6 @@
                 for j in range(2):
                     out[e, layer : layer + 1, block(j)] = fresh[layer, 2 * half + j, at : at + 1, :]
 
-    hear(1)
-    tell(2)
     first_sweep(0)
     layers2 = [fresh_copies(0), fresh_copies(1)]
     for copy in layers2[0]:
@@ -408,8 +408,6 @@
     outer = edge_copies(outer_out, outer_in, outer_corner, outer_sem, outer_corner_sem, 19, faces=False)
     for copy in outer:
         copy.start()
-    hear(2)
-    tell(3)
     first_sweep(1)
     for layer in range(2):
         compact = as_row(fresh[layer, 1, :, LANES - 1 : LANES])
@@ -448,10 +446,10 @@
         copy.wait_recv()
     second_sweep(0, outer_in, outer_corner, ())
 
-    hear(3)
     load_order.wait()
 
     def target_group(i):
+        i = jnp.where(i < FAR - 1, i + 1, jnp.where(i == FAR - 1, 0, i))
         return jnp.where(i % 2 == 1, groups // 2 - (i + 1) // 2, groups - groups // 2 + i // 2) % groups
 
     def pick(j, first, count):
@@ -474,7 +472,9 @@
 
         lax.fori_loop(begin, end, body, 0)
 
-    spread(0, FAR, 0, EARLY, 0)
+    spread(0, FAR - 1, 0, EARLY, 0)
+    hear(3)
+    spread(FAR - 1, FAR, 0, EARLY, 0)
 
     for copy in inner[:3]:
         copy.wait_recv()

time: 58.6 us -> 57.8 us (0.986)
  Pallas kernels: 57.2 us -> 56.4 us
    pallas_call x1, Pallas kernels: 56.4 us -> 55.5 us  [on_device(): pl.pallas_call(functools.partial(kernel, slabs, sections, mechs), out_sha...]
where the time goes in v4:
time: 57.8 us; the launch traced here: 57.7 us
  Pallas kernels  56.4 us (98%)
  between operations  1.29 us (2%)
    pallas_call x1, Pallas kernels, on_device(): pl.pallas_call(functools.partial(kernel, slabs, sections, mechs), out_sha...  55.5 us

profile of v4, /device:TPU:1, one launch (start us, length us, event | category | flops | bytes accessed | tf_op | source)
XLA Modules:
  0.0 57.7 jit_solution(16796132390511785692)
XLA Ops:
  1.3 55.5 %shard_map.86 = (f32[128,8,128]{2,1,0:T(8,128)S(1)}, f32[16,8,128]{2,1,0:T(8,128)S(1)}) custom-call(f32[2,128,512]{2,1,0:T(8,128)} %bitcast.7, f32[2,128,512]{2,1,0:T(8,128)} %bitcast.8, f32[2,128]{1,0:T(2,128)} %bitcast.10, s32[1,128]{1,0:T(1,128)} %bitcast.11, s32[1,128]{1,0:T(1,128)} %order_in.1, s32[1,1]{1,0:T(1,128)S(6)} %copy.11.active_in, ...), custom_call_target="tpu_custom_call" | custom-call | tf_op jit(solution)/shard_map/pallas_call | solution.py:578
  56.8 0.8 %shard_map.87 = (f32[128,8,128]{2,1,0:T(8,128)}, f32[16,8,128]{2,1,0:T(8,128)}) custom-call(f32[128,8,128]{2,1,0:T(8,128)S(1)} %get-tuple-element.6.stress_ref, f32[16,8,128]{2,1,0:T(8,128)S(1)} %get-tuple-element.7.strain_ref), custom_call_target="tpu_custom_call" | custom-call | tf_op jit(solution)/shard_map/pallas_call | solution.py:646
